TPU v7x, 256 devices: a whole 4x4x8 slice. The times are simulated.
256 devices in a mesh: lat: 32 (over x, z_lo, y), lon: 8 (over z_hi, core).
Axes of the slice: x: 4, y: 4, z: 8 (z_hi: 4, z_lo: 2; z = z_hi * 2 + z_lo), core: 2. Of those that a mesh axis runs over, the one named last changes fastest.
Arguments:
- grid_in: bfloat16 [128, 1440, 256], P('lat', 'lon'), may hold values from -6 to 6
- grid_cotangent: bfloat16 [128, 1440, 256], P('lat', 'lon'), may hold values from -6 to 6
- support_filter: float32 [128, 5, 1440], P('lat'), may hold values from -2.5 to 2.5
- band_half: int32 [128], P('lat'), may hold values from 1 to 2, as said below
- w_mix: bfloat16 [256, 256], replicated, may hold values from -0.375 to 0.375
- norm_gain: float32 [256], replicated, may hold values from 0.5 to 1.5
- w_up: bfloat16 [256, 1024], replicated, may hold values from -0.375 to 0.375
- w_down: bfloat16 [1024, 256], replicated, may hold values from -0.1875 to 0.1875
Outputs:
- grid_out: bfloat16 [128, 1440, 256], P('lat', 'lon')
- grid_grad: bfloat16 [128, 1440, 256], P('lat', 'lon')
- mix_grad: float32 [256, 256], replicated
- gain_grad: float32 [256], replicated
- up_grad: float32 [256, 1024], replicated
- down_grad: float32 [1024, 256], replicated
Inputs may be any that keep to these rules, and one draw needn't show every extreme that they name: `band_half`: cycles within 4 of either pole have the full support 2.
All inputs are finite; a program needn't handle non-finite values.
Results may differ from a plain program's by a relative error of at most 0.023.
Values may be sent and summed in bfloat16 or wider, within the bound.
A program may use at most 64 MiB of HBM per device.

v0:
```python
import jax
import jax.numpy as jnp
from jax import lax
from jax.sharding import PartitionSpec as P

SQRT_TWO_PI = 0.7978845608028654
CUBIC = 0.044715


def with_halo(cells, sides, width):
    for axis, dim in sides:
        count = lax.axis_size(axis)
        ends = count - 1
        head = lax.slice_in_dim(cells, 0, width, axis=dim)
        tail = lax.slice_in_dim(cells, cells.shape[dim] - width, cells.shape[dim], axis=dim)
        cells = jnp.concatenate(
            [
                lax.ppermute(tail, axis, [(i, (i + 1) % count) for i in range(ends)]),
                cells,
                lax.ppermute(head, axis, [((i + 1) % count, i) for i in range(ends)]),
            ],
            axis=dim,
        )
    return cells


def gelu_tanh(values):
    tanh_arg = SQRT_TWO_PI * (values + CUBIC * values * values * values)
    return 0.5 * values * (1.0 + jnp.tanh(tanh_arg))


def gelu_slope(values):
    tanh_arg = SQRT_TWO_PI * (values + CUBIC * values * values * values)
    tangent = jnp.tanh(tanh_arg)
    return 0.5 * (1.0 + tangent) + 0.5 * values * (1.0 - tangent * tangent) * SQRT_TWO_PI * (
        1.0 + 3.0 * CUBIC * values * values
    )


def inner_rows(left_side, right_side):
    return lax.dot_general(
        left_side, right_side, (((0,), (0,)), ((), ())), preferred_element_type=jnp.float32
    )


def times_transpose(left_side, right_side):
    return lax.dot_general(
        left_side, right_side, (((1,), (1,)), ((), ())), preferred_element_type=jnp.float32
    )


def fourier_values(positions, mode_ids, length):
    half_len = length // 2
    frequency = jnp.where(mode_ids < half_len, mode_ids, mode_ids - half_len)
    phase_int = positions[:, None] * frequency[None, :] % length
    angle_rad = phase_int.astype(jnp.float32) * (2.0 * 3.141592653589793 / length)
    return jnp.where((mode_ids < half_len)[None, :], jnp.cos(angle_rad), jnp.sin(angle_rad))


def forward_table(positions, mode_ids, length):
    return fourier_values(positions, mode_ids, length).astype(jnp.bfloat16)


def inverse_table(mode_ids, positions, length):
    fourier = fourier_values(positions, mode_ids, length)
    weight = jnp.where(mode_ids == 0, 1.0, 2.0) / length
    return (jnp.transpose(fourier) * weight[:, None]).astype(jnp.bfloat16)


def masked_filter(support_filter, band_half):
    reach_rows = (support_filter.shape[1] - 1) // 2
    tap_offsets = jnp.arange(support_filter.shape[1], dtype=jnp.int32) - reach_rows
    inside = jnp.abs(tap_offsets)[None, :] <= band_half[:, None]
    return jnp.where(inside[:, :, None], support_filter, 0.0)


def band_forward(padded, filtered):
    lat_rows = filtered.shape[0]
    running = jnp.zeros((padded.shape[0], lat_rows, padded.shape[2]), jnp.float32)
    for tap_index in range(filtered.shape[1]):
        coeffs = jnp.transpose(filtered[:, tap_index, :])
        running = running + coeffs[:, :, None] * padded[:, tap_index : tap_index + lat_rows].astype(
            jnp.float32
        )
    return running.astype(jnp.bfloat16)


def band_adjoint(grad_padded, filter_padded, lat_rows):
    tap_count = filter_padded.shape[1]
    reach_rows = (tap_count - 1) // 2
    running = jnp.zeros((grad_padded.shape[0], lat_rows, grad_padded.shape[2]), jnp.float32)
    for tap_index in range(tap_count):
        begin_at = 2 * reach_rows - tap_index
        coeffs = jnp.transpose(filter_padded[begin_at : begin_at + lat_rows, tap_index, :])
        running = running + coeffs[:, :, None] * grad_padded[
            :, begin_at : begin_at + lat_rows
        ].astype(jnp.float32)
    return running.astype(jnp.bfloat16)


def tail_pass(flat_in, flat_conv, cotangent, w_mix, norm_gain, w_up, w_down):
    mixed = jnp.dot(flat_conv, w_mix, preferred_element_type=jnp.float32)
    stream = (flat_in.astype(jnp.float32) + mixed).astype(jnp.bfloat16)
    stream_f = stream.astype(jnp.float32)
    inverse = lax.rsqrt(jnp.mean(stream_f * stream_f, axis=-1, keepdims=True) + 1e-06)
    normed = stream_f * inverse
    scaled = (normed * norm_gain).astype(jnp.bfloat16)
    before = jnp.dot(scaled, w_up, preferred_element_type=jnp.float32)
    hidden = gelu_tanh(before).astype(jnp.bfloat16)
    result = (stream_f + jnp.dot(hidden, w_down, preferred_element_type=jnp.float32)).astype(
        jnp.bfloat16
    )
    d_hidden = times_transpose(cotangent, w_down)
    down_term = inner_rows(hidden, cotangent)
    d_before = (d_hidden * gelu_slope(before)).astype(jnp.bfloat16)
    up_term = inner_rows(scaled, d_before)
    d_scaled = times_transpose(d_before, w_up)
    gain_term = jnp.sum(d_scaled * normed, axis=0)
    gained = d_scaled * norm_gain
    d_stream = cotangent.astype(jnp.float32) + inverse * (
        gained - normed * jnp.mean(gained * normed, axis=-1, keepdims=True)
    )
    d_stream16 = d_stream.astype(jnp.bfloat16)
    mix_term = inner_rows(flat_conv, d_stream16)
    d_conv = times_transpose(d_stream16, w_mix).astype(jnp.bfloat16)
    return (result, d_stream, d_conv, (mix_term, gain_term, up_term, down_term))


def local(grid_in, grid_cotangent, support_filter, band_half, w_mix, norm_gain, w_up, w_down):
    lat_rows, lon_cols, channel_count = grid_in.shape
    lon_count = lon_cols * lax.axis_size("lon")
    reach_rows = (support_filter.shape[1] - 1) // 2
    filtered = masked_filter(support_filter, band_half)
    all_cols = jnp.arange(lon_count, dtype=jnp.int32)
    forward_full = forward_table(all_cols, all_cols, lon_count)
    inverse_full = inverse_table(all_cols, all_cols, lon_count)
    turned = lax.all_to_all(grid_in, "lon", split_axis=2, concat_axis=1, tiled=True)
    spectra = jnp.einsum(
        "jlc,lk->kjc", turned, forward_full, preferred_element_type=jnp.float32
    ).astype(jnp.bfloat16)
    padded = with_halo(spectra, (("lat", 1),), reach_rows)
    banded = band_forward(padded, filtered)
    conv_turned = jnp.einsum(
        "kic,kl->ilc", banded, inverse_full, preferred_element_type=jnp.float32
    ).astype(jnp.bfloat16)
    conv_grid = lax.all_to_all(conv_turned, "lon", split_axis=1, concat_axis=2, tiled=True)
    flat_rows = lat_rows * lon_cols
    result, d_stream, d_conv, grad_terms = tail_pass(
        grid_in.reshape(flat_rows, channel_count),
        conv_grid.reshape(flat_rows, channel_count),
        grid_cotangent.reshape(flat_rows, channel_count),
        w_mix,
        norm_gain,
        w_up,
        w_down,
    )
    grid_out = result.reshape(lat_rows, lon_cols, channel_count)
    d_conv = d_conv.reshape(lat_rows, lon_cols, channel_count)
    d_turned = lax.all_to_all(d_conv, "lon", split_axis=2, concat_axis=1, tiled=True)
    d_banded = jnp.einsum(
        "ilc,kl->kic", d_turned, inverse_full, preferred_element_type=jnp.float32
    ).astype(jnp.bfloat16)
    grad_padded = with_halo(d_banded, (("lat", 1),), reach_rows)
    filter_padded = with_halo(filtered.astype(jnp.bfloat16), (("lat", 0),), reach_rows).astype(
        filtered.dtype
    )
    d_spectra = band_adjoint(grad_padded, filter_padded, lat_rows)
    back_turned = jnp.einsum(
        "kjc,lk->jlc", d_spectra, forward_full, preferred_element_type=jnp.float32
    )
    back_grid = lax.all_to_all(
        back_turned.astype(jnp.bfloat16), "lon", split_axis=1, concat_axis=2, tiled=True
    ).astype(back_turned.dtype)
    grid_grad = (d_stream.reshape(lat_rows, lon_cols, channel_count) + back_grid).astype(
        jnp.bfloat16
    )
    mix_term, gain_term, up_term, down_term = grad_terms
    summed = lax.psum((mix_term, gain_term, up_term, down_term), ("lat", "lon"))
    norm_scale = float(lat_rows * lax.axis_size("lat") * lon_count) ** (-0.5)
    return (
        grid_out,
        grid_grad,
        summed[0] * norm_scale,
        summed[1] * norm_scale,
        summed[2] * norm_scale,
        summed[3] * norm_scale,
    )


def solution(mesh):
    return jax.shard_map(
        local,
        mesh=mesh,
        in_specs=(
            P("lat", "lon", None),
            P("lat", "lon", None),
            P("lat", None, None),
            P("lat"),
            P(),
            P(),
            P(),
            P(),
        ),
        out_specs=(P("lat", "lon", None), P("lat", "lon", None), P(), P(), P(), P()),
        check_vma=False,
    )
```

profile of v0, /device:TPU:1, one launch (start us, length us, event | category | flops | bytes accessed | tf_op | source)
XLA Modules:
  0.0 492.5 jit_solution(4062318949159286942)
XLA Ops:
  7.2 2.1 copy.33
  9.3 10.0 %all-to-all-start = ((bf16[4,180,256]{1,0,2:T(4,128)(2,1)}), bf16[4,180,256]{1,0,2:T(4,128)(2,1)S(1)}, u32[]{:S(2)}, u32[]{:S(2)}) async-start(bf16[4,180,256]{1,0,2:T(4,128)(2,1)} %copy.33), calls=%async_computation | async-start | bytes 1048576 | tf_op jit(solution)/shard_map/all_to_all | solution.py:137
  19.2 0.7 broadcast_compare_fusion
  20.0 1.0 fusion.46
  21.0 0.7 fusion.49
  21.6 3.8 collective-permute-start.2
  25.4 1.3 collective-permute-start.3
  26.8 40.6 %multiply_convert_fusion.14 = bf16[1440,1440]{1,0:T(8,128)(2,1)} fusion(f32[1440]{0:T(1024)S(1)} %select_multiply_fusion, s32[1440]{0:T(1024)S(1)} %add_select_fusion.2, pred[1440]{0:T(1024)(128)(4,1)S(1)} %iota_compare_fusion.1), kind=kLoop, calls=%fused_computation.10.clone.1.clone.1 | loop fusion | flops 24883200 | bytes 4160160
  67.4 38.6 %select_convert_fusion.7 = bf16[1440,1440]{1,0:T(8,128)(2,1)} fusion(s32[1440]{0:T(1024)S(1)} %add_select_fusion.2, pred[1440]{0:T(1024)(128)(4,1)S(1)} %iota_compare_fusion.1), kind=kLoop, calls=%fused_computation.6.clone.1.clone.1 | loop fusion | flops 22809600 | bytes 4154400
  106.1 0.3 copy.35
  106.4 0.5 all_to_all.47
  106.9 3.2 fusion.13
  110.2 4.0 collective-permute-start
  114.2 1.3 collective-permute-start.1
  115.5 2.4 collective-permute-done
  117.9 3.8 collective-permute-done.1
  121.7 0.3 add_convert_fusion.1
  122.0 0.8 fusion.11
  122.9 1.7 copy.36
  124.5 1.8 reshape.124
  126.3 8.6 %all-to-all-start.1 = ((bf16[8,2,11520]{2,1,0:T(2,128)(2,1)}), bf16[8,2,11520]{2,1,0:T(2,128)(2,1)S(1)}, u32[]{:S(2)}, u32[]{:S(2)}) async-start(bf16[8,2,11520]{2,1,0:T(2,128)(2,1)} %reshape.124), calls=%async_computation.1 | async-start | bytes 737280 | tf_op jit(solution)/shard_map/all_to_all | solution.py:146
  134.9 40.6 %multiply_convert_fusion.13 = bf16[1440,1440]{1,0:T(8,128)(2,1)} fusion(f32[1440]{0:T(1024)S(1)} %select_multiply_fusion, s32[1440]{0:T(1024)S(1)} %add_select_fusion.2, pred[1440]{0:T(1024)(128)(4,1)S(1)} %iota_compare_fusion.1), kind=kLoop, calls=%fused_computation.10.clone.clone.1 | loop fusion | flops 24883200 | bytes 4160160
  175.7 0.8 reshape.110
  176.5 1.6 convert_bitcast_fusion.5
  178.1 0.8 reshape.125
  178.9 2.5 copy.37
  181.4 0.4 reshape.108
  181.8 0.4 multiply_reduce_fusion.2
  182.3 0.6 fusion.44
  183.0 2.2 fusion.20
  185.1 1.7 fusion.43
  186.8 1.2 multiply_reduce_fusion
  188.0 0.3 multiply_add_fusion.1
  188.3 0.3 convolution_convert_fusion
  188.6 1.0 reshape.111
  189.6 3.0 fusion.23
  192.7 1.1 copy.39
  193.8 7.2 %all-to-all-start.2 = ((bf16[4,180,256]{1,0,2:T(4,128)(2,1)}), bf16[4,180,256]{1,0,2:T(4,128)(2,1)S(1)}, u32[]{:S(2)}, u32[]{:S(2)}) async-start(bf16[4,180,256]{1,0,2:T(4,128)(2,1)} %copy.39), calls=%async_computation.2 | async-start | bytes 1048576 | tf_op jit(solution)/shard_map/all_to_all | solution.py:159
  201.0 0.9 copy.45
  201.9 1.0 fusion.28
  202.9 3.9 fusion.45
  206.9 83.0 %psum.29 = f32[256]{0:T(256)S(1)} all-reduce(f32[256]{0:T(256)S(1)} %copy-done.15), channel_id=1, replica_groups=mesh['lat'=32,'lon'=8] {'lat','lon'}, use_global_device_ids=true, to_apply=%region_4.5 | all-reduce | flops 256 | bytes 2048 | tf_op jit(solution)/shard_map/psum | solution.py:178
  290.0 0.3 copy.41
  290.3 0.5 all_to_all.54
  290.8 3.8 fusion.10
  294.7 1.3 collective-permute-start.4
  296.0 4.0 collective-permute-start.5
  300.0 0.6 broadcast_multiply_fusion.4
  300.6 1.6 collective-permute-done.4
  302.2 0.4 collective-permute-done.5
  302.6 0.3 add_convert_fusion
  302.9 38.7 %fusion.12 = f32[1440,128]{0,1:S(1)} fusion(bf16[1440,128]{0,1:T(8,128)(2,1)S(1)} %bitcast.123, s32[1440]{0:T(1024)S(1)} %copy-done.12, pred[1440]{0:T(1024)(128)(4,1)S(1)} %copy-done.14), kind=kOutput, calls=%fused_computation.20 | convolution fusion | flops 553651200 | bytes 1113120
  341.7 1.7 copy.42
  343.4 1.8 reshape.126
  345.1 6.9 %all-to-all-start.3 = ((bf16[8,2,11520]{2,1,0:T(2,128)(2,1)}), bf16[8,2,11520]{2,1,0:T(2,128)(2,1)S(1)}, u32[]{:S(2)}, u32[]{:S(2)}) async-start(bf16[8,2,11520]{2,1,0:T(2,128)(2,1)} %reshape.126), calls=%async_computation.3 | async-start | bytes 737280 | tf_op jit(solution)/shard_map/all_to_all | solution.py:171
  352.0 123.0 %all-reduce.3.cloned.1.call-done = (f32[256,256]{1,0:T(8,128)}, f32[256,1024]{1,0:T(8,128)}, f32[1024,256]{1,0:T(8,128)}) async-done(((f32[256,256]{1,0:T(8,128)}, f32[256,1024]{1,0:T(8,128)}, f32[1024,256]{1,0:T(8,128)}), (f32[256,256]{1,0:T(8,128)}, f32[256,1024]{1,0:T(8,128)}, f32[1024,256]{1,0:T(8,128)})) %all-reduce.3.cloned.1.call-update) | async-done | bytes 2359312 | tf_op jit(solution)/shard_map/psum | solution.py:178
  475.0 1.8 broadcast_multiply_fusion.2
  476.8 2.3 broadcast_multiply_fusion
  479.1 1.1 broadcast_multiply_fusion.1
  480.2 0.8 reshape.127
  481.0 2.3 copy.43
  483.3 0.3 copy.44
  483.6 1.2 add_convert_fusion.2
  484.8 0.9 copy.46
  (67 shorter events, 0.9 us)
Async XLA Ops:
  7.2 175.1 %copy-start = (bf16[256,1024]{1,0:T(8,128)(2,1)S(1)}, bf16[256,1024]{1,0:T(8,128)(2,1)}, u32[]{:S(2)}) copy-start(bf16[256,1024]{1,0:T(8,128)(2,1)} %param.14) | copy-start | bytes 1572868
  9.3 96.7 %all-to-all-start = ((bf16[4,180,256]{1,0,2:T(4,128)(2,1)}), bf16[4,180,256]{1,0,2:T(4,128)(2,1)S(1)}, u32[]{:S(2)}, u32[]{:S(2)}) async-start(bf16[4,180,256]{1,0,2:T(4,128)(2,1)} %copy.33), calls=%async_computation | async-start | bytes 1048576 | tf_op jit(solution)/shard_map/all_to_all | solution.py:137
  21.6 154.9 %collective-permute-start.2 = (bf16[2,5,1440]{2,0,1:T(2,128)(2,1)}, bf16[2,5,1440]{2,0,1:T(2,128)(2,1)}, u32[]{:S(2)}, u32[]{:S(2)}) collective-permute-start(bf16[2,5,1440]{2,0,1:T(2,128)(2,1)} %get-tuple-element.45), channel_id=1, source_target_pairs={{0,8},{8,16},{16,24},{24,32},{32,40},{40,48},{48,56},{56,64},{64,7... | collective-permute-start | bytes 86408 | tf_op jit(solution)/shard_map/ppermute | solution.py:18
  25.4 151.1 %collective-permute-start.3 = (bf16[2,5,1440]{2,0,1:T(2,128)(2,1)}, bf16[2,5,1440]{2,0,1:T(2,128)(2,1)}, u32[]{:S(2)}, u32[]{:S(2)}) collective-permute-start(bf16[2,5,1440]{2,0,1:T(2,128)(2,1)} %get-tuple-element.46), channel_id=1, source_target_pairs={{8,0},{16,8},{24,16},{32,24},{40,32},{48,40},{56,48},{64,56},{72,6... | collective-permute-start | bytes 86408 | tf_op jit(solution)/shard_map/ppermute | solution.py:20
  26.7 108.1 %copy-start.11 = (s32[1440]{0:T(1024)}, s32[1440]{0:T(1024)S(1)}, u32[]{:S(2)}) copy-start(s32[1440]{0:T(1024)S(1)} %add_select_fusion.2) | copy-start | bytes 17284
  26.8 108.1 %copy-start.13 = (pred[1440]{0:T(1024)(128)(4,1)}, pred[1440]{0:T(1024)(128)(4,1)S(1)}, u32[]{:S(2)}) copy-start(pred[1440]{0:T(1024)(128)(4,1)S(1)} %iota_compare_fusion.1) | copy-start | bytes 4324
  106.9 15.1 %slice-start = ((s8[4423680]{0:T(1024)(128)(4,1)}), s8[4194304]{0:T(1024)(128)(4,1)S(1)}, s32[]{:S(2)}) async-start(s8[4423680]{0:T(1024)(128)(4,1)} %bitcast.110), calls=%async_computation.5 | async-start | bytes 8388608
  106.9 15.1 %slice-start.1 = ((s8[4423680]{0:T(1024)(128)(4,1)}), s8[229376]{0:T(1024)(128)(4,1)S(1)}, s32[]{:S(2)}) async-start(s8[4423680]{0:T(1024)(128)(4,1)} %bitcast.110), calls=%async_computation.6 | async-start | bytes 458752
  110.2 7.7 %collective-permute-start = (bf16[1440,2,32]{0,2,1:T(8,128)(2,1)S(1)}, bf16[1440,2,32]{0,2,1:T(8,128)(2,1)S(1)}, u32[]{:S(2)}, u32[]{:S(2)}) collective-permute-start(bf16[1440,2,32]{0,2,1:T(8,128)(2,1)S(1)} %get-tuple-element.33), channel_id=1, source_target_pairs={{0,8},{8,16},{16,24},{24,32},{32,40},{40,48},{48,56},{56,64},{64,7... | collective-permute-start | bytes 552968 | tf_op jit(solution)/shard_map/ppermute | solution.py:18
  114.2 7.5 %collective-permute-start.1 = (bf16[1440,2,32]{0,2,1:T(8,128)(2,1)S(1)}, bf16[1440,2,32]{0,2,1:T(8,128)(2,1)S(1)}, u32[]{:S(2)}, u32[]{:S(2)}) collective-permute-start(bf16[1440,2,32]{0,2,1:T(8,128)(2,1)S(1)} %get-tuple-element.34), channel_id=1, source_target_pairs={{8,0},{16,8},{24,16},{32,24},{40,32},{48,40},{56,48},{64,56},{72,6... | collective-permute-start | bytes 552968 | tf_op jit(solution)/shard_map/ppermute | solution.py:20
  126.3 51.8 %all-to-all-start.1 = ((bf16[8,2,11520]{2,1,0:T(2,128)(2,1)}), bf16[8,2,11520]{2,1,0:T(2,128)(2,1)S(1)}, u32[]{:S(2)}, u32[]{:S(2)}) async-start(bf16[8,2,11520]{2,1,0:T(2,128)(2,1)} %reshape.124), calls=%async_computation.1 | async-start | bytes 737280 | tf_op jit(solution)/shard_map/all_to_all | solution.py:146
  134.9 40.6 %copy-start.3 = (bf16[4,180,256]{2,0,1:T(4,128)(2,1)S(1)}, bf16[4,180,256]{2,0,1:T(4,128)(2,1)}, u32[]{:S(2)}) copy-start(bf16[4,180,256]{2,0,1:T(4,128)(2,1)} %param.8) | copy-start | bytes 1105924
  134.9 40.7 %copy-start.6 = (bf16[4,180,256]{2,0,1:T(4,128)(2,1)S(1)}, bf16[4,180,256]{2,0,1:T(4,128)(2,1)}, u32[]{:S(2)}) copy-start(bf16[4,180,256]{2,0,1:T(4,128)(2,1)} %param.9) | copy-start | bytes 1105924
  175.7 6.1 %copy-start.5 = (bf16[256,256]{1,0:T(8,128)(2,1)S(1)}, bf16[256,256]{1,0:T(8,128)(2,1)}, u32[]{:S(2)}) copy-start(bf16[256,256]{1,0:T(8,128)(2,1)} %param.12) | copy-start | bytes 393220
  178.1 4.2 copy-start.10
  181.8 1.1 copy-start.2
  181.8 1.1 copy-start.16
  183.0 2.2 copy-start.1
  193.8 96.1 %all-to-all-start.2 = ((bf16[4,180,256]{1,0,2:T(4,128)(2,1)}), bf16[4,180,256]{1,0,2:T(4,128)(2,1)S(1)}, u32[]{:S(2)}, u32[]{:S(2)}) async-start(bf16[4,180,256]{1,0,2:T(4,128)(2,1)} %copy.39), calls=%async_computation.2 | async-start | bytes 1048576 | tf_op jit(solution)/shard_map/all_to_all | solution.py:159
  201.0 274.1 %all-reduce.3.cloned.1.call-start = ((), (), s32[]{:S(2)}) async-start(), calls=%async_computation.4 | async-start | bytes 4718592 | tf_op jit(solution)/shard_map/psum | solution.py:178
  202.9 4.0 copy-start.15
  290.8 11.8 %copy-start.7 = (f32[1440,4]{0,1:T(4,128)S(1)}, f32[1440,4]{0,1:T(4,128)}, u32[]{:S(2)}) copy-start(f32[1440,4]{0,1:T(4,128)} %get-tuple-element.37) | copy-start | bytes 69124
  290.8 11.8 %copy-start.8 = (f32[1440,4]{0,1:T(4,128)S(1)}, f32[1440,4]{0,1:T(4,128)}, u32[]{:S(2)}) copy-start(f32[1440,4]{0,1:T(4,128)} %get-tuple-element.38) | copy-start | bytes 69124
  290.8 11.8 %copy-start.9 = (f32[1440,4]{0,1:T(4,128)S(1)}, f32[1440,4]{0,1:T(4,128)}, u32[]{:S(2)}) copy-start(f32[1440,4]{0,1:T(4,128)} %get-tuple-element.39) | copy-start | bytes 69124
  294.6 8.3 %copy-start.12 = (s32[1440]{0:T(1024)S(1)}, s32[1440]{0:T(1024)}, u32[]{:S(2)}) copy-start(s32[1440]{0:T(1024)} %copy-done.11) | copy-start | bytes 17284
  294.6 8.3 %copy-start.14 = (pred[1440]{0:T(1024)(128)(4,1)S(1)}, pred[1440]{0:T(1024)(128)(4,1)}, u32[]{:S(2)}) copy-start(pred[1440]{0:T(1024)(128)(4,1)} %copy-done.13) | copy-start | bytes 4324
  294.7 7.5 %collective-permute-start.4 = (bf16[1440,2,32]{0,2,1:T(8,128)(2,1)S(1)}, bf16[1440,2,32]{0,2,1:T(8,128)(2,1)S(1)}, u32[]{:S(2)}, u32[]{:S(2)}) collective-permute-start(bf16[1440,2,32]{0,2,1:T(8,128)(2,1)S(1)} %get-tuple-element.31), channel_id=1, source_target_pairs={{8,0},{16,8},{24,16},{32,24},{40,32},{48,40},{56,48},{64,56},{72,6... | collective-permute-start | bytes 552968 | tf_op jit(solution)/shard_map/ppermute | solution.py:20
  296.0 6.6 %collective-permute-start.5 = (bf16[1440,2,32]{0,2,1:T(8,128)(2,1)S(1)}, bf16[1440,2,32]{0,2,1:T(8,128)(2,1)S(1)}, u32[]{:S(2)}, u32[]{:S(2)}) collective-permute-start(bf16[1440,2,32]{0,2,1:T(8,128)(2,1)S(1)} %get-tuple-element.32), channel_id=1, source_target_pairs={{0,8},{8,16},{16,24},{24,32},{32,40},{40,48},{48,56},{56,64},{64,7... | collective-permute-start | bytes 552968 | tf_op jit(solution)/shard_map/ppermute | solution.py:18
  345.1 135.1 %all-to-all-start.3 = ((bf16[8,2,11520]{2,1,0:T(2,128)(2,1)}), bf16[8,2,11520]{2,1,0:T(2,128)(2,1)S(1)}, u32[]{:S(2)}, u32[]{:S(2)}) async-start(bf16[8,2,11520]{2,1,0:T(2,128)(2,1)} %reshape.126), calls=%async_computation.3 | async-start | bytes 737280 | tf_op jit(solution)/shard_map/all_to_all | solution.py:171
  475.0 4.1 copy-start.4
Sparse Core Ops, SparseCore 0:
  208.1 266.8 all-reduce.2
where the time goes:
time: 494 us; the launch traced here: 493 us
  other arithmetic  131 us (27%)
  waiting for transfers between devices  131 us (27%)
  blocking collectives  83 us (17%)
  matrix products  60.6 us (12%)
  starting transfers between devices  48.3 us (10%)
  local copies, waits for them, and re-layouts  23.7 us (5%)
  between operations  14.6 us (3%)
    psum x1, waiting for transfers between devices, local(): summed = lax.psum((mix_term, gain_term, up_term, down_term), ('lat', 'lon'))  123 us
    unnamed x4, other arithmetic  120 us
    psum x1, blocking collectives, local(): summed = lax.psum((mix_term, gain_term, up_term, down_term), ('lat', 'lon'))  83 us
    unnamed x4, matrix products  46.4 us
    ppermute x3, starting transfers between devices, with_halo(): lax.ppermute(tail, axis, [(i, (i + 1) % count) for i in range(ends)])  11.8 us
    all_to_all x1, starting transfers between devices, local(): lax.all_to_all(grid_in, 'lon', split_axis=2, concat_axis=1, tiled=True)  9.97 us
  transfers between devices with their start and end apart: 11, of which 5 were waited for; matrix products, arithmetic and copies ran while one was open for 39% of the time, Pallas kernels for 0%

commit v1 on v0

v1 whole, which is shorter than its diff:
```python
import jax
import jax.numpy as jnp
import ml_dtypes
import numpy as np
from jax import lax
from jax.experimental import pallas as pl
from jax.experimental.pallas import tpu as pltpu
from jax.sharding import PartitionSpec as P

SQRT_TWO_PI = 0.7978845608028654
CUBIC = 0.044715
MESH = pl.DeviceIdType.MESH
BF16 = jnp.bfloat16
F32 = jnp.float32

LAT = 32
LON = 8
PAIRS = LON // 2
ROWS = 4
COLS = 180
BLK = 192
NLON = LON * COLS
MODES = LON * BLK
CH = 256
HID = 1024
TAPS = 5
FLAT = ROWS * BLK


def fourier_tables():
    modes = np.arange(NLON)
    freq = np.where(modes < NLON // 2, modes, modes - NLON // 2)
    phase = (freq[:, None] * modes[None, :]) % NLON
    angle = phase * (2.0 * np.pi / NLON)
    values = np.where((modes < NLON // 2)[:, None], np.cos(angle), np.sin(angle))
    table = np.zeros((MODES, LON, BLK), np.float32)
    table[:NLON, :, :COLS] = values.reshape(NLON, LON, COLS)
    table = table.reshape(MODES, MODES).astype(ml_dtypes.bfloat16)
    return table, np.ascontiguousarray(table.T)


def expansion():
    fwd = np.zeros((32, TAPS, ROWS, 32), np.float32)
    bwd = np.zeros((64, TAPS, ROWS, 32), np.float32)
    for w in range(TAPS):
        for i in range(ROWS):
            fwd[8 * i + w, w, i] = 1.0
            bwd[8 * (i + w) + 4 - w, w, i] = 1.0
    fwd = fwd.reshape(32, TAPS * 128)
    bwd = bwd.reshape(64, TAPS * 128)
    return fwd.astype(ml_dtypes.bfloat16), bwd.astype(ml_dtypes.bfloat16)


def dot(a, b):
    return jnp.dot(a, b, preferred_element_type=F32)


def dot_rows(a, b):
    return lax.dot_general(a, b, (((0,), (0,)), ((), ())), preferred_element_type=F32)


def dot_transpose(a, b):
    return lax.dot_general(a, b, (((1,), (1,)), ((), ())), preferred_element_type=F32)


def lanes_of(shape):
    return lax.broadcasted_iota(jnp.int32, shape, 1)


def turn_groups(parts):
    lane = lanes_of(parts[0].shape)
    low = lane < 64
    a, b, c, d = parts
    a, c = jnp.where(low, a, pltpu.roll(c, 64, 1)), jnp.where(low, pltpu.roll(a, 64, 1), c)
    b, d = jnp.where(low, b, pltpu.roll(d, 64, 1)), jnp.where(low, pltpu.roll(b, 64, 1), d)
    even = (lane % 64) < 32
    a, b = jnp.where(even, a, pltpu.roll(b, 32, 1)), jnp.where(even, pltpu.roll(a, 96, 1), b)
    c, d = jnp.where(even, c, pltpu.roll(d, 32, 1)), jnp.where(even, pltpu.roll(c, 96, 1), d)
    return a, b, c, d


def kernel(
    gin, cot, filt, band, wmix, gain, wup, wdown, efwd, ebwd, fwd_hbm, inv_hbm,
    out, grad, mix_o, gain_o, up_o, down_o,
    fwd, inv, gpad, cpad, send, recv, hsend, hrecv, halo, fstage, fown, fhalo, coef, dcoef,
    spec, banded, conv, field, stream, scaled, before, dhid, hidden, dbef, dstream, dstream16,
    tsem, ssem, rsem, hssem, hrsem, fssem, frsem,
):
    lat = lax.axis_index("lat")
    me = lax.axis_index("lon")
    pair = me // 2
    after = lax.rem(lat + 1, LAT)
    ahead = lax.rem(lat + LAT - 1, LAT)

    get_fwd = pltpu.make_async_copy(fwd_hbm, fwd, tsem.at[0])
    get_inv = pltpu.make_async_copy(inv_hbm, inv, tsem.at[1])
    get_fwd.start()
    get_inv.start()

    barrier = pltpu.get_barrier_semaphore()
    for s in range(1, LON):
        pl.semaphore_signal(barrier, inc=1, device_id={"lon": lax.rem(me + s, LON)}, device_id_type=MESH)
    for there in (after, ahead):
        pl.semaphore_signal(barrier, inc=1, device_id={"lat": there}, device_id_type=MESH)

    def exchange(ph, q):
        return pltpu.make_async_remote_copy(
            src_ref=send.at[ph, q], dst_ref=recv.at[ph, me],
            send_sem=ssem.at[ph, q], recv_sem=rsem.at[ph, me],
            device_id={"lon": q}, device_id_type=MESH,
        )

    def arrived(ph, p):
        pltpu.make_async_remote_copy(
            src_ref=send.at[ph, p], dst_ref=recv.at[ph, p],
            send_sem=ssem.at[ph, p], recv_sem=rsem.at[ph, p],
            device_id={"lon": p}, device_id_type=MESH,
        ).wait_recv()

    def halo_copy(ph, side, g):
        return pltpu.make_async_remote_copy(
            src_ref=hsend.at[ph, side, g], dst_ref=hrecv.at[ph, side, g],
            send_sem=hssem.at[ph, side, g], recv_sem=hrsem.at[ph, side, g],
            device_id={"lat": after if side == 0 else ahead}, device_id_type=MESH,
        )

    def filter_copy(side):
        return pltpu.make_async_remote_copy(
            src_ref=fown.at[pl.ds(16 if side == 0 else 0, 16)], dst_ref=fhalo.at[side],
            send_sem=fssem.at[side], recv_sem=frsem.at[side],
            device_id={"lat": after if side == 0 else ahead}, device_id_type=MESH,
        )

    def pack(src, ph):
        @pl.loop(0, BLK // 64)
        def _(step):
            at = step * 64
            for half in range(2):
                parts = [
                    src[pl.ds(i * BLK + at, 64), half * 128 : half * 128 + 128].astype(F32)
                    for i in range(ROWS)
                ]
                for g, block in enumerate(turn_groups(parts)):
                    send[ph, half * 4 + g, pl.ds(at, 64), :] = block.astype(BF16)

    def unpack(ph, put):
        @pl.loop(0, BLK // 64)
        def _(step):
            at = step * 64
            for half in range(2):
                parts = [recv[ph, half * 4 + g, pl.ds(at, 64), :].astype(F32) for g in range(4)]
                for i, block in enumerate(turn_groups(parts)):
                    put(i, at, half, block)

    def start_exchange(ph):
        for s in range(1, LON):
            exchange(ph, lax.rem(me + s, LON)).start()

    def keep_own(ph):
        recv[ph, me] = send[ph, me]

    def gather_with_halo(ph, hp):
        for s in range(PAIRS):
            g = lax.rem(pair + s, PAIRS)
            if s == 0:
                arrived(ph, 2 * pair + 1 - (me - 2 * pair))
            else:
                arrived(ph, 2 * g)
                arrived(ph, 2 * g + 1)

            @pl.loop(0, BLK // 64)
            def _(step):
                at = pl.ds(step * 64, 64)
                one = recv[ph, 2 * g, at, :].astype(F32)
                two = recv[ph, 2 * g + 1, at, :].astype(F32)
                low = lanes_of(one.shape) < 64
                hsend[hp, 0, g, at, :] = jnp.where(low, pltpu.roll(one, 64, 1), two).astype(BF16)
                hsend[hp, 1, g, at, :] = jnp.where(low, one, pltpu.roll(two, 64, 1)).astype(BF16)

            halo_copy(hp, 0, g).start()
            halo_copy(hp, 1, g).start()
        for s in range(PAIRS):
            g = lax.rem(pair + s, PAIRS)
            halo_copy(hp, 0, g).wait_recv()
            halo_copy(hp, 1, g).wait_recv()

            @pl.loop(0, BLK // 64)
            def _(step):
                at = pl.ds(step * 64, 64)
                one = hrecv[hp, 0, g, at, :].astype(F32)
                two = hrecv[hp, 1, g, at, :].astype(F32)
                low = lanes_of(one.shape) < 64
                halo[2 * g, at, :] = jnp.where(low, one, pltpu.roll(two, 64, 1)).astype(BF16)
                halo[2 * g + 1, at, :] = jnp.where(low, pltpu.roll(one, 64, 1), two).astype(BF16)

    def to_modes(ph):
        @pl.loop(0, MODES // 512)
        def _(step):
            at = pl.ds(pl.multiple_of(step * 512, 512), 512)
            both = jnp.concatenate(
                [recv[ph].reshape(MODES, 128), halo[...].reshape(MODES, 128)], axis=1
            )
            spec[at, :] = dot(fwd[at, :], both)

    def band_sum(weights):
        @pl.loop(0, MODES // 64)
        def _(step):
            at = pl.ds(pl.multiple_of(step * 64, 64), 64)
            own = spec[at, 0:128]
            edge = spec[at, 128:256]
            lane = lanes_of(own.shape)
            half = pltpu.roll(own, 64, 1)
            windows = (
                jnp.where(lane < 64, edge, half),
                jnp.where(lane < 32, pltpu.roll(edge, 96, 1), pltpu.roll(own, 32, 1)),
                own,
                jnp.where(lane >= 96, pltpu.roll(edge, 32, 1), pltpu.roll(own, 96, 1)),
                jnp.where(lane >= 64, edge, half),
            )
            total = windows[0] * weights[at, 0:128]
            for w in range(1, TAPS):
                total = total + windows[w] * weights[at, w * 128 : w * 128 + 128]
            banded[at, :] = total.astype(BF16)

    def to_grid_and_send(ph):
        for s in range(PAIRS):
            g = lax.rem(pair + 1 + s, PAIRS)
            rows = pl.ds(pl.multiple_of(g * 2 * BLK, 2 * BLK), 2 * BLK)
            block = dot(inv[rows, :], banded[...]).astype(BF16)
            send[ph, 2 * g] = block[0:BLK]
            send[ph, 2 * g + 1] = block[BLK:]
            if s < PAIRS - 1:
                exchange(ph, 2 * g).start()
                exchange(ph, 2 * g + 1).start()
            else:
                exchange(ph, 2 * pair + 1 - (me - 2 * pair)).start()
        keep_own(ph)

    gpad[...] = jnp.zeros_like(gpad)
    cpad[...] = jnp.zeros_like(cpad)
    for i in range(ROWS):
        gpad[i * BLK : i * BLK + COLS, :] = gin[i]
        cpad[i * BLK : i * BLK + COLS, :] = cot[i]
    pack(gpad, 0)
    pl.semaphore_wait(barrier, LON - 1 + 2)
    start_exchange(0)
    keep_own(0)

    fstage[...] = jnp.zeros_like(fstage)
    tap = lax.broadcasted_iota(jnp.int32, (TAPS, NLON), 0)
    mode = lax.broadcasted_iota(jnp.int32, (TAPS, NLON), 1)
    scale = jnp.where(mode == 0, 1.0 / NLON, 2.0 / NLON)
    for i in range(ROWS):
        reaches = lat * ROWS + i + tap - 2
        keep = (jnp.abs(tap - 2) <= band[i]) & (reaches >= 0) & (reaches < LAT * ROWS)
        fstage[8 * i : 8 * i + TAPS, 0:NLON] = jnp.where(keep, filt[i] * scale, 0.0)
    fown[...] = fstage[...].astype(BF16)
    filter_copy(0).start()
    filter_copy(1).start()

    @pl.loop(0, MODES // 256)
    def _(step):
        at = pl.ds(pl.multiple_of(step * 256, 256), 256)
        coef[at, :] = dot_rows(fown[:, at], efwd[...])

    dhid[...] = dot_transpose(cpad[...], wdown[...])

    get_fwd.wait()
    gather_with_halo(0, 0)
    to_modes(0)
    band_sum(coef)
    get_inv.wait()
    to_grid_and_send(1)

    filter_copy(0).wait()
    filter_copy(1).wait()

    @pl.loop(0, MODES // 256)
    def _(step):
        at = pl.ds(pl.multiple_of(step * 256, 256), 256)
        rows = jnp.concatenate([fhalo[0, :, at], fown[:, at], fhalo[1, :, at]], axis=0)
        dcoef[at, :] = dot_rows(rows, ebwd[...])

    for s in range(1, LON):
        arrived(1, lax.rem(me + s, LON))

    def put_conv(i, at, half, block):
        conv[pl.ds(i * BLK + at, 64), half * 128 : half * 128 + 128] = block.astype(BF16)

    unpack(1, put_conv)

    field[...] = dot(conv[...], wmix[...])

    @pl.loop(0, FLAT // 64)
    def _(step):
        at = pl.ds(step * 64, 64)
        s16 = (gpad[at, :].astype(F32) + field[at, :]).astype(BF16)
        stream[at, :] = s16
        sf = s16.astype(F32)
        inverse = lax.rsqrt(jnp.mean(sf * sf, axis=-1, keepdims=True) + 1e-06)
        scaled[at, :] = (sf * inverse * gain[...]).astype(BF16)

    before[...] = dot(scaled[...], wup[...])

    @pl.loop(0, FLAT // 16)
    def _(step):
        at = pl.ds(step * 16, 16)
        u = before[at, :]
        u2 = u * u
        tangent = jnp.tanh(u * (SQRT_TWO_PI + (SQRT_TWO_PI * CUBIC) * u2))
        h = 0.5 * u
        hidden[at, :] = (h + h * tangent).astype(BF16)
        slope = (0.5 + 0.5 * tangent) + (h * (1.0 - tangent * tangent)) * (
            SQRT_TWO_PI + (3.0 * SQRT_TWO_PI * CUBIC) * u2
        )
        dbef[at, :] = (dhid[at, :] * slope).astype(BF16)

    field[...] = dot_transpose(dbef[...], wup[...])
    gain_o[...] = jnp.zeros_like(gain_o)

    @pl.loop(0, FLAT // 64)
    def _(step):
        at = pl.ds(step * 64, 64)
        sf = stream[at, :].astype(F32)
        inverse = lax.rsqrt(jnp.mean(sf * sf, axis=-1, keepdims=True) + 1e-06)
        normed = sf * inverse
        d_scaled = field[at, :]
        gain_o[...] += jnp.sum(d_scaled * normed, axis=0, keepdims=True)
        gained = d_scaled * gain[...]
        ds = cpad[at, :].astype(F32) + inverse * (
            gained - normed * jnp.mean(gained * normed, axis=-1, keepdims=True)
        )
        dstream[at, :] = ds
        dstream16[at, :] = ds.astype(BF16)

    field[...] = dot_transpose(dstream16[...], wmix[...])
    pack(field, 2)
    start_exchange(2)
    keep_own(2)

    field[...] = dot(hidden[...], wdown[...])
    for i in range(ROWS):
        at = slice(i * BLK, i * BLK + BLK)
        out[i] = (stream[at, :].astype(F32) + field[at, :])[0:COLS].astype(BF16)
    mix_o[...] = dot_rows(conv[...], dstream16[...])
    up_o[...] = dot_rows(scaled[...], dbef[...])
    down_o[...] = dot_rows(hidden[...], cpad[...])

    gather_with_halo(2, 1)
    to_modes(2)
    band_sum(dcoef)
    to_grid_and_send(3)
    for s in range(1, LON):
        arrived(3, lax.rem(me + s, LON))

    def put_field(i, at, half, block):
        rows = pl.ds(i * BLK + at, 64)
        lanes = slice(half * 128, half * 128 + 128)
        field[rows, lanes] = block + dstream[rows, lanes]

    unpack(3, put_field)
    for i in range(ROWS):
        grad[i] = field[i * BLK : i * BLK + BLK, :][0:COLS].astype(BF16)

    for ph in range(4):
        for s in range(1, LON):
            exchange(ph, lax.rem(me + s, LON)).wait_send()
    for hp in range(2):
        for g in range(PAIRS):
            halo_copy(hp, 0, g).wait_send()
            halo_copy(hp, 1, g).wait_send()


def local(grid_in, grid_cotangent, support_filter, band_half, w_mix, norm_gain, w_up, w_down):
    table, turned = fourier_tables()
    efwd, ebwd = expansion()
    vmem = pl.BlockSpec(memory_space=pltpu.VMEM)
    smem = pl.BlockSpec(memory_space=pltpu.SMEM)
    anywhere = pl.BlockSpec(memory_space=pl.ANY)
    outs = pl.pallas_call(
        kernel,
        out_shape=(
            jax.ShapeDtypeStruct((ROWS, COLS, CH), BF16),
            jax.ShapeDtypeStruct((ROWS, COLS, CH), BF16),
            jax.ShapeDtypeStruct((CH, CH), F32),
            jax.ShapeDtypeStruct((1, CH), F32),
            jax.ShapeDtypeStruct((CH, HID), F32),
            jax.ShapeDtypeStruct((HID, CH), F32),
        ),
        in_specs=[vmem, vmem, vmem, smem] + [vmem] * 6 + [anywhere] * 2,
        out_specs=[vmem] * 6,
        scratch_shapes=[
            pltpu.VMEM((MODES, MODES), BF16),
            pltpu.VMEM((MODES, MODES), BF16),
            pltpu.VMEM((FLAT, CH), BF16),
            pltpu.VMEM((FLAT, CH), BF16),
            pltpu.VMEM((4, LON, BLK, 128), BF16),
            pltpu.VMEM((4, LON, BLK, 128), BF16),
            pltpu.VMEM((2, 2, PAIRS, BLK, 128), BF16),
            pltpu.VMEM((2, 2, PAIRS, BLK, 128), BF16),
            pltpu.VMEM((LON, BLK, 128), BF16),
            pltpu.VMEM((32, MODES), F32),
            pltpu.VMEM((32, MODES), BF16),
            pltpu.VMEM((2, 16, MODES), BF16),
            pltpu.VMEM((MODES, TAPS * 128), F32),
            pltpu.VMEM((MODES, TAPS * 128), F32),
            pltpu.VMEM((MODES, 256), F32),
            pltpu.VMEM((MODES, 128), BF16),
            pltpu.VMEM((FLAT, CH), BF16),
            pltpu.VMEM((FLAT, CH), F32),
            pltpu.VMEM((FLAT, CH), BF16),
            pltpu.VMEM((FLAT, CH), BF16),
            pltpu.VMEM((FLAT, HID), F32),
            pltpu.VMEM((FLAT, HID), F32),
            pltpu.VMEM((FLAT, HID), BF16),
            pltpu.VMEM((FLAT, HID), BF16),
            pltpu.VMEM((FLAT, CH), F32),
            pltpu.VMEM((FLAT, CH), BF16),
            pltpu.SemaphoreType.DMA((2,)),
            pltpu.SemaphoreType.DMA((4, LON)),
            pltpu.SemaphoreType.DMA((4, LON)),
            pltpu.SemaphoreType.DMA((2, 2, PAIRS)),
            pltpu.SemaphoreType.DMA((2, 2, PAIRS)),
            pltpu.SemaphoreType.DMA((2,)),
            pltpu.SemaphoreType.DMA((2,)),
        ],
        compiler_params=pltpu.CompilerParams(
            collective_id=0, has_side_effects=True, vmem_limit_bytes=60 * 1024 * 1024
        ),
        cost_estimate=pl.CostEstimate(flops=4_700_000_000, bytes_accessed=14_000_000, transcendentals=800_000),
    )(
        grid_in, grid_cotangent, support_filter, band_half, w_mix, norm_gain.reshape(1, CH), w_up, w_down,
        jnp.asarray(efwd), jnp.asarray(ebwd), jnp.asarray(table), jnp.asarray(turned),
    )
    grid_out, grid_grad, mix_term, gain_term, up_term, down_term = outs
    summed = lax.psum((mix_term, gain_term.reshape(CH), up_term, down_term), ("lat", "lon"))
    norm_scale = float(LAT * ROWS * NLON) ** (-0.5)
    return (grid_out, grid_grad) + tuple(term * norm_scale for term in summed)


def solution(mesh):
    return jax.shard_map(
        local,
        mesh=mesh,
        in_specs=(
            P("lat", "lon", None),
            P("lat", "lon", None),
            P("lat", None, None),
            P("lat"),
            P(),
            P(),
            P(),
            P(),
        ),
        out_specs=(P("lat", "lon", None), P("lat", "lon", None), P(), P(), P(), P()),
        check_vma=False,
    )
```

time: 494 us -> 375 us (0.76)
  other arithmetic: 131 us -> 6.87 us
  Pallas kernels: 0 us -> 89.9 us
  matrix products: 60.6 us -> 0 us
  starting transfers between devices: 48.3 us -> 0.04 us
  waiting for transfers between devices: 131 us -> 178 us
  local copies, waits for them, and re-layouts: 23.7 us -> 8.9 us
  blocking collectives: 83 us -> 76.6 us
    unnamed x4 -> x0, other arithmetic: 120 us -> none
    pallas_call x0 -> x1, Pallas kernels: none -> 89.9 us  [local(): pl.pallas_call(kernel, out_shape=(jax.ShapeDtypeStruct((ROWS, COLS, CH),...]
    psum x1, waiting for transfers between devices: 123 us -> 178 us  [local(): lax.psum((mix_term, gain_term.reshape(CH), up_term, down_term), ('lat', '...]
    unnamed x4 -> x0, matrix products: 46.4 us -> none
    all_to_all x4 -> x0, starting transfers between devices: 32.6 us -> none  [the longest x1 9.97 us: local(): lax.all_to_all(grid_in, 'lon', split_axis=2, concat_axis=1, tiled=True)]
    ppermute x6 -> x0, starting transfers between devices: 15.7 us -> none  [the longest x3 11.8 us: with_halo(): lax.ppermute(tail, axis, [(i, (i + 1) % count) for i in range(ends)])]
    dot_general x9 -> x0, matrix products: 14.2 us -> none  [the longest x3 6.58 us: inner_rows(): lax.dot_general(left_side, right_side, (((0,), (0,)), ((), ())), preferre...]
    ppermute x6 -> x0, waiting for transfers between devices: 8.18 us -> none  [the longest x3 5.43 us: with_halo(): lax.ppermute(head, axis, [((i + 1) % count, i) for i in range(ends)])]
  transfers between devices with their start and end apart: 11 -> 1, of which waited for: 5 -> 1; matrix products, arithmetic and copies ran while one was open for 39% -> 1% of each run, Pallas kernels for 0% -> 0%
where the time goes in v1:
time: 375 us; the launch traced here: 374 us
  waiting for transfers between devices  178 us (47%)
  Pallas kernels  89.9 us (24%)
  blocking collectives  76.6 us (20%)
  between operations  14 us (4%)
  local copies, waits for them, and re-layouts  8.9 us (2%)
  other arithmetic  6.87 us (2%)
    psum x1, waiting for transfers between devices, local(): lax.psum((mix_term, gain_term.reshape(CH), up_term, down_term), ('lat', '...  178 us
    pallas_call x1, Pallas kernels, local(): pl.pallas_call(kernel, out_shape=(jax.ShapeDtypeStruct((ROWS, COLS, CH),...  89.9 us
    psum x1, blocking collectives, local(): lax.psum((mix_term, gain_term.reshape(CH), up_term, down_term), ('lat', '...  76.6 us
    unnamed x5, local copies, waits for them, and re-layouts  8.9 us
  transfers between devices with their start and end apart: 1, of which 1 were waited for; matrix products, arithmetic and copies ran while one was open for 1% of the time, Pallas kernels for 0%

profile of v1, /device:TPU:1, one launch (start us, length us, event | category | flops | bytes accessed | tf_op | source)
XLA Modules:
  0.0 373.9 jit_solution(9079490138374773781)
XLA Ops:
  7.2 0.0 all-reduce.3.cloned.1.call-start
  7.2 1.8 copy.18.gin
  9.0 1.8 copy.19.cot
  10.7 1.6 copy.20.filt
  12.4 89.9 %shard_map.163 = (bf16[4,180,256]{2,1,0:T(8,128)(2,1)}, bf16[4,180,256]{2,1,0:T(8,128)(2,1)}, f32[256,256]{1,0:T(8,128)}, f32[1,256]{1,0:T(1,128)}, f32[256,1024]{1,0:T(8,128)}, /*index=5*/f32[1024,256]{1,0:T(8,128)}) custom-call(bf16[4,180,256]{2,1,0:T(8,128)(2,1)} %copy.18.gin, bf16[4,180,256]{2,1,0:T(8,128)(2,1)} %copy.19.cot, f32[4,5,1440]{2,1,0:T(8,128)} %copy.20.filt, ...), custom_call_target="tpu_custom_call" | custom-call | flops 4700000256 | bytes 14000000 | tf_op jit(solution)/shard_map/pallas_call | solution.py:380
  102.3 0.0 all-reduce.3.cloned.1.call-update
  102.3 1.9 copy.21
  104.2 1.9 copy.22
  106.0 76.6 %psum.29 = f32[256]{0:T(256)S(1)} all-reduce(f32[256]{0:T(256)} %bitcast.2), channel_id=1, replica_groups=mesh['lat'=32,'lon'=8] {'lat','lon'}, use_global_device_ids=true, to_apply=%region_1.0 | all-reduce | flops 256 | bytes 2048 | tf_op jit(solution)/shard_map/psum | solution.py:436
  182.6 0.6 broadcast_multiply_fusion.3
  183.2 177.6 %all-reduce.3.cloned.1.call-done = (f32[256,256]{1,0:T(8,128)}, f32[256,1024]{1,0:T(8,128)}, f32[1024,256]{1,0:T(8,128)}) async-done(((f32[256,256]{1,0:T(8,128)}, f32[256,1024]{1,0:T(8,128)}, f32[1024,256]{1,0:T(8,128)}), (f32[256,256]{1,0:T(8,128)}, f32[256,1024]{1,0:T(8,128)}, f32[1024,256]{1,0:T(8,128)})) %all-reduce.3.cloned.1.call-update) | async-done | bytes 2359312 | tf_op jit(solution)/shard_map/psum | solution.py:436
  360.7 1.7 broadcast_multiply_fusion.2
  362.4 2.3 broadcast_multiply_fusion.1
  364.7 2.3 broadcast_multiply_fusion
Async XLA Ops:
  7.2 353.6 %all-reduce.3.cloned.1.call-start = ((), (), s32[]{:S(2)}) async-start(), calls=%async_computation | async-start | bytes 4718592 | tf_op jit(solution)/shard_map/psum | solution.py:436
Sparse Core Ops, SparseCore 0:
  102.4 258.2 all-reduce.2

commit v2 on v1

--- a/solution.py
+++ b/solution.py
@@ -26,6 +26,15 @@
 TAPS = 5
 FLAT = ROWS * BLK
 
+HALF = 2304
+XA, YA = 320, 80
+YB, XB = 256, 64
+B_AT = 4 * XA
+GAIN_AT = 2 * HALF
+TILE = 16
+Z_ROWS = 32
+NORM_SCALE = float(LAT * ROWS * NLON) ** (-0.5)
+
 
 def fourier_tables():
     modes = np.arange(NLON)
@@ -84,13 +93,29 @@
     out, grad, mix_o, gain_o, up_o, down_o,
     fwd, inv, gpad, cpad, send, recv, hsend, hrecv, halo, fstage, fown, fhalo, coef, dcoef,
     spec, banded, conv, field, stream, scaled, before, dhid, hidden, dbef, dstream, dstream16,
-    tsem, ssem, rsem, hssem, hrsem, fssem, frsem,
+    gsum, part, csend, crecv, a1s, a1r, b1s, b1r, a1, b1, a2s, a2r, b2s, b2r, zf, zs, zr, zall, a3, b3, fin,
+    tsem, ssem, rsem, hssem, hrsem, fssem, frsem, cssem, crsem, xssem, xrsem, yssem, yrsem, zssem, zrsem,
 ):
     lat = lax.axis_index("lat")
     me = lax.axis_index("lon")
     pair = me // 2
     after = lax.rem(lat + 1, LAT)
     ahead = lax.rem(lat + LAT - 1, LAT)
+    core = me - 2 * pair
+    x = lat // 8
+    z_lo = lat // 4 - 2 * x
+    y = lat - 8 * x - 4 * z_lo
+    z = 2 * pair + z_lo
+    mine = pl.multiple_of(core * HALF, HALF)
+
+    def x_peer(to):
+        return {"lat": to * 8 + z_lo * 4 + y}
+
+    def y_peer(to):
+        return {"lat": x * 8 + z_lo * 4 + to}
+
+    def z_peer(to):
+        return {"lat": x * 8 + (to - to // 2 * 2) * 4 + y, "lon": to // 2 * 2 + core}
 
     get_fwd = pltpu.make_async_copy(fwd_hbm, fwd, tsem.at[0])
     get_inv = pltpu.make_async_copy(inv_hbm, inv, tsem.at[1])
@@ -102,6 +127,11 @@
         pl.semaphore_signal(barrier, inc=1, device_id={"lon": lax.rem(me + s, LON)}, device_id_type=MESH)
     for there in (after, ahead):
         pl.semaphore_signal(barrier, inc=1, device_id={"lat": there}, device_id_type=MESH)
+    for s in range(1, 4):
+        pl.semaphore_signal(barrier, inc=1, device_id=x_peer(lax.rem(x + s, 4)), device_id_type=MESH)
+        pl.semaphore_signal(barrier, inc=1, device_id=y_peer(lax.rem(y + s, 4)), device_id_type=MESH)
+    for s in range(1, 8):
+        pl.semaphore_signal(barrier, inc=1, device_id=z_peer(lax.rem(z + s, 8)), device_id_type=MESH)
 
     def exchange(ph, q):
         return pltpu.make_async_remote_copy(
@@ -236,13 +266,195 @@
                 exchange(ph, 2 * pair + 1 - (me - 2 * pair)).start()
         keep_own(ph)
 
+    def core_copy(kind):
+        src, dst = (csend, crecv) if kind == 0 else (fin.at[pl.ds(mine, HALF)], fin.at[pl.ds(mine, HALF)])
+        return pltpu.make_async_remote_copy(
+            src_ref=src, dst_ref=dst, send_sem=cssem.at[kind], recv_sem=crsem.at[kind],
+            device_id={"lon": me + 1 - 2 * core}, device_id_type=MESH,
+        )
+
+    def core_arrived():
+        at = pl.multiple_of((1 - core) * HALF, HALF)
+        pltpu.make_async_remote_copy(
+            src_ref=fin.at[pl.ds(at, HALF)], dst_ref=fin.at[pl.ds(at, HALF)],
+            send_sem=cssem.at[1], recv_sem=crsem.at[1],
+            device_id={"lon": me + 1 - 2 * core}, device_id_type=MESH,
+        ).wait_recv()
+
+    def x_copy(kind, to, own):
+        src, dst = (
+            (a1s.at[to], a1r.at[own]),
+            (b2s.at[to], b2r.at[own]),
+            (b3.at[pl.ds(own * XB, XB)], b3.at[pl.ds(own * XB, XB)]),
+            (a3, fin.at[pl.ds(mine + own * XA, XA)]),
+        )[kind]
+        return src, dst
+
+    def y_copy(kind, to, own):
+        src, dst = (
+            (b1s.at[to], b1r.at[own]),
+            (a2s.at[to], a2r.at[own]),
+            (a3.at[pl.ds(own * YA, YA)], a3.at[pl.ds(own * YA, YA)]),
+            (b3, fin.at[pl.ds(mine + B_AT + own * YB, YB)]),
+        )[kind]
+        return src, dst
+
+    def z_copy(kind, to, own):
+        src, dst = (
+            (zs.at[pl.ds(to * Z_ROWS, Z_ROWS)], zr.at[own]),
+            (zall.at[pl.ds(own * Z_ROWS, Z_ROWS)], zall.at[pl.ds(own * Z_ROWS, Z_ROWS)]),
+        )[kind]
+        return src, dst
+
+    rings = {
+        "x": (x, 4, x_copy, x_peer, xssem, xrsem),
+        "y": (y, 4, y_copy, y_peer, yssem, yrsem),
+        "z": (z, 8, z_copy, z_peer, zssem, zrsem),
+    }
+
+    def ring_copy(axis, kind, to, own):
+        _, _, copy, peer, send_sems, recv_sems = rings[axis]
+        src, dst = copy(kind, to, own)
+        return pltpu.make_async_remote_copy(
+            src_ref=src, dst_ref=dst, send_sem=send_sems.at[kind, to], recv_sem=recv_sems.at[kind, own],
+            device_id=peer(to), device_id_type=MESH,
+        )
+
+    def ring_start(axis, kind):
+        here, count = rings[axis][:2]
+        for s in range(1, count):
+            ring_copy(axis, kind, lax.rem(here + s, count), here).start()
+
+    def ring_arrived(axis, kind):
+        here, count = rings[axis][:2]
+        for s in range(1, count):
+            there = lax.rem(here + s, count)
+            ring_copy(axis, kind, there, there).wait_recv()
+
+    def ring_sent(axis, kind):
+        here, count = rings[axis][:2]
+        for s in range(1, count):
+            ring_copy(axis, kind, lax.rem(here + s, count), here).wait_send()
+
+    def others(ref, here, count, rows):
+        total = ref[lax.rem(here + 1, count), rows, :].astype(F32)
+        for s in range(2, count):
+            total = total + ref[lax.rem(here + s, count), rows, :].astype(F32)
+        return total
+
+    gain_rows = pl.ds(GAIN_AT, TILE)
+
+    def sum_over_cores_start():
+        theirs = pl.multiple_of((1 - core) * HALF, HALF)
+
+        @pl.loop(0, HALF // 128)
+        def _(step):
+            csend[pl.ds(step * 128, 128), :] = part[pl.ds(theirs + step * 128, 128), :].astype(BF16)
+
+        csend[HALF:, :] = part[gain_rows, :].astype(BF16)
+        core_copy(0).start()
+
+    def scatter_first():
+        core_copy(0).wait_recv()
+
+        def one(at, put, where):
+            v = part[pl.ds(mine + at, 64), :] + crecv[pl.ds(at, 64), :].astype(F32)
+            part[pl.ds(mine + at, 64), :] = v
+            put[where[0], pl.ds(where[1], 64), :] = v.astype(BF16)
+
+        for to in range(4):
+
+            @pl.loop(0, XA // 64)
+            def _(step):
+                one(to * XA + step * 64, a1s, (to, step * 64))
+
+            @pl.loop(0, YB // 64)
+            def _(step):
+                one(B_AT + to * YB + step * 64, b1s, (to, step * 64))
+
+        g = part[gain_rows, :] + crecv[HALF:, :].astype(F32)
+        part[gain_rows, :] = g
+        for to in range(4):
+            a1s[to, XA:, :] = g.astype(BF16)
+        ring_start("x", 0)
+        ring_start("y", 0)
+
+    def scatter_second():
+        ring_arrived("x", 0)
+        ring_arrived("y", 0)
+
+        @pl.loop(0, XA // 64)
+        def _(step):
+            rows = pl.ds(step * 64, 64)
+            a1[rows, :] = part[pl.ds(mine + x * XA + step * 64, 64), :] + others(a1r, x, 4, rows)
+
+        a1[XA:, :] = part[gain_rows, :] + others(a1r, x, 4, pl.ds(XA, TILE))
+
+        @pl.loop(0, YB // 64)
+        def _(step):
+            rows = pl.ds(step * 64, 64)
+            b1[rows, :] = part[pl.ds(mine + B_AT + y * YB + step * 64, 64), :] + others(b1r, y, 4, rows)
+
+        for to in range(4):
+            a2s[to, 0:YA, :] = a1[to * YA : to * YA + YA, :].astype(BF16)
+            a2s[to, YA:, :] = a1[XA:, :].astype(BF16)
+            b2s[to] = b1[to * XB : to * XB + XB, :].astype(BF16)
+        ring_start("y", 1)
+        ring_start("x", 1)
+
+    def scatter_z():
+        ring_arrived("y", 1)
+        ring_arrived("x", 1)
+        zf[YA + TILE + XB :, :] = jnp.zeros((8 * Z_ROWS - YA - TILE - XB, 128), F32)
+        zf[0:YA, :] = a1[pl.ds(y * YA, YA), :] + others(a2r, y, 4, pl.ds(0, YA))
+        zf[YA : YA + TILE, :] = a1[XA:, :] + others(a2r, y, 4, pl.ds(YA, TILE))
+        zf[YA + TILE : YA + TILE + XB, :] = b1[pl.ds(x * XB, XB), :] + others(b2r, x, 4, pl.ds(0, XB))
+        zs[...] = zf[...].astype(BF16)
+        ring_start("z", 0)
+
+    def gather_z():
+        ring_arrived("z", 0)
+        rows = pl.ds(pl.multiple_of(z * Z_ROWS, Z_ROWS), Z_ROWS)
+        zall[rows, :] = (zf[rows, :] + others(zr, z, 8, pl.ds(0, Z_ROWS))).astype(BF16)
+        ring_start("z", 1)
+
+    def gather_first():
+        ring_arrived("z", 1)
+        a3[pl.ds(y * YA, YA), :] = zall[0:YA, :]
+        b3[pl.ds(x * XB, XB), :] = zall[YA + TILE : YA + TILE + XB, :]
+        ring_start("y", 2)
+        ring_start("x", 2)
+
+    def gather_second():
+        ring_arrived("y", 2)
+        ring_arrived("x", 2)
+        ring_start("x", 3)
+        ring_start("y", 3)
+        fin[pl.ds(mine + x * XA, XA), :] = a3[...]
+        fin[pl.ds(mine + B_AT + y * YB, YB), :] = b3[...]
+
+    def gather_over_cores():
+        ring_arrived("x", 3)
+        ring_arrived("y", 3)
+        core_copy(1).start()
+
+    def write_sums():
+        core_arrived()
+        for h in range(2):
+            lanes = slice(h * 128, h * 128 + 128)
+            mix_o[:, lanes] = fin[h * 256 : h * 256 + 256, :].astype(F32) * NORM_SCALE
+            down_o[:, lanes] = fin[2560 + h * 1024 : 2560 + h * 1024 + 1024, :].astype(F32) * NORM_SCALE
+            gain_o[:, lanes] = zall[YA : YA + TILE, :].astype(F32)[h : h + 1, :] * NORM_SCALE
+        for h in range(8):
+            up_o[:, h * 128 : h * 128 + 128] = fin[512 + h * 256 : 768 + h * 256, :].astype(F32) * NORM_SCALE
+
     gpad[...] = jnp.zeros_like(gpad)
     cpad[...] = jnp.zeros_like(cpad)
     for i in range(ROWS):
         gpad[i * BLK : i * BLK + COLS, :] = gin[i]
         cpad[i * BLK : i * BLK + COLS, :] = cot[i]
     pack(gpad, 0)
-    pl.semaphore_wait(barrier, LON - 1 + 2)
+    pl.semaphore_wait(barrier, LON - 1 + 2 + 3 + 3 + 7)
     start_exchange(0)
     keep_own(0)
 
@@ -316,7 +528,7 @@
         dbef[at, :] = (dhid[at, :] * slope).astype(BF16)
 
     field[...] = dot_transpose(dbef[...], wup[...])
-    gain_o[...] = jnp.zeros_like(gain_o)
+    gsum[...] = jnp.zeros_like(gsum)
 
     @pl.loop(0, FLAT // 64)
     def _(step):
@@ -325,7 +537,7 @@
         inverse = lax.rsqrt(jnp.mean(sf * sf, axis=-1, keepdims=True) + 1e-06)
         normed = sf * inverse
         d_scaled = field[at, :]
-        gain_o[...] += jnp.sum(d_scaled * normed, axis=0, keepdims=True)
+        gsum[...] += jnp.sum(d_scaled * normed, axis=0, keepdims=True)
         gained = d_scaled * gain[...]
         ds = cpad[at, :].astype(F32) + inverse * (
             gained - normed * jnp.mean(gained * normed, axis=-1, keepdims=True)
@@ -342,14 +554,30 @@
     for i in range(ROWS):
         at = slice(i * BLK, i * BLK + BLK)
         out[i] = (stream[at, :].astype(F32) + field[at, :])[0:COLS].astype(BF16)
-    mix_o[...] = dot_rows(conv[...], dstream16[...])
-    up_o[...] = dot_rows(scaled[...], dbef[...])
-    down_o[...] = dot_rows(hidden[...], cpad[...])
+    term = dot_rows(conv[...], dstream16[...])
+    for h in range(2):
+        part[h * 256 : h * 256 + 256, :] = term[:, h * 128 : h * 128 + 128]
+    term = dot_rows(scaled[...], dbef[...])
+    for h in range(8):
+        part[512 + h * 256 : 768 + h * 256, :] = term[:, h * 128 : h * 128 + 128]
+    term = dot_rows(hidden[...], cpad[...])
+    for h in range(2):
+        part[2560 + h * 1024 : 3584 + h * 1024, :] = term[:, h * 128 : h * 128 + 128]
+    part[gain_rows, :] = jnp.zeros((TILE, 128), F32)
+    for h in range(2):
+        part[GAIN_AT + h : GAIN_AT + h + 1, :] = gsum[:, h * 128 : h * 128 + 128]
+    sum_over_cores_start()
 
     gather_with_halo(2, 1)
+    scatter_first()
     to_modes(2)
+    scatter_second()
     band_sum(dcoef)
+    scatter_z()
     to_grid_and_send(3)
+    gather_z()
+    gather_first()
+    gather_second()
     for s in range(1, LON):
         arrived(3, lax.rem(me + s, LON))
 
@@ -362,6 +590,16 @@
     for i in range(ROWS):
         grad[i] = field[i * BLK : i * BLK + BLK, :][0:COLS].astype(BF16)
 
+    gather_over_cores()
+    write_sums()
+
+    core_copy(0).wait_send()
+    core_copy(1).wait_send()
+    for kind in range(4):
+        ring_sent("x", kind)
+        ring_sent("y", kind)
+    for kind in range(2):
+        ring_sent("z", kind)
     for ph in range(4):
         for s in range(1, LON):
             exchange(ph, lax.rem(me + s, LON)).wait_send()
@@ -416,6 +654,27 @@
             pltpu.VMEM((FLAT, HID), BF16),
             pltpu.VMEM((FLAT, CH), F32),
             pltpu.VMEM((FLAT, CH), BF16),
+            pltpu.VMEM((1, CH), F32),
+            pltpu.VMEM((2 * HALF + TILE, 128), F32),
+            pltpu.VMEM((HALF + TILE, 128), BF16),
+            pltpu.VMEM((HALF + TILE, 128), BF16),
+            pltpu.VMEM((4, XA + TILE, 128), BF16),
+            pltpu.VMEM((4, XA + TILE, 128), BF16),
+            pltpu.VMEM((4, YB, 128), BF16),
+            pltpu.VMEM((4, YB, 128), BF16),
+            pltpu.VMEM((XA + TILE, 128), F32),
+            pltpu.VMEM((YB, 128), F32),
+            pltpu.VMEM((4, YA + TILE, 128), BF16),
+            pltpu.VMEM((4, YA + TILE, 128), BF16),
+            pltpu.VMEM((4, XB, 128), BF16),
+            pltpu.VMEM((4, XB, 128), BF16),
+            pltpu.VMEM((8 * Z_ROWS, 128), F32),
+            pltpu.VMEM((8 * Z_ROWS, 128), BF16),
+            pltpu.VMEM((8, Z_ROWS, 128), BF16),
+            pltpu.VMEM((8 * Z_ROWS, 128), BF16),
+            pltpu.VMEM((4 * YA, 128), BF16),
+            pltpu.VMEM((4 * XB, 128), BF16),
+            pltpu.VMEM((2 * HALF, 128), BF16),
             pltpu.SemaphoreType.DMA((2,)),
             pltpu.SemaphoreType.DMA((4, LON)),
             pltpu.SemaphoreType.DMA((4, LON)),
@@ -423,6 +682,14 @@
             pltpu.SemaphoreType.DMA((2, 2, PAIRS)),
             pltpu.SemaphoreType.DMA((2,)),
             pltpu.SemaphoreType.DMA((2,)),
+            pltpu.SemaphoreType.DMA((2,)),
+            pltpu.SemaphoreType.DMA((2,)),
+            pltpu.SemaphoreType.DMA((4, 4)),
+            pltpu.SemaphoreType.DMA((4, 4)),
+            pltpu.SemaphoreType.DMA((4, 4)),
+            pltpu.SemaphoreType.DMA((4, 4)),
+            pltpu.SemaphoreType.DMA((2, 8)),
+            pltpu.SemaphoreType.DMA((2, 8)),
         ],
         compiler_params=pltpu.CompilerParams(
             collective_id=0, has_side_effects=True, vmem_limit_bytes=60 * 1024 * 1024
@@ -433,9 +700,7 @@
         jnp.asarray(efwd), jnp.asarray(ebwd), jnp.asarray(table), jnp.asarray(turned),
     )
     grid_out, grid_grad, mix_term, gain_term, up_term, down_term = outs
-    summed = lax.psum((mix_term, gain_term.reshape(CH), up_term, down_term), ("lat", "lon"))
-    norm_scale = float(LAT * ROWS * NLON) ** (-0.5)
-    return (grid_out, grid_grad) + tuple(term * norm_scale for term in summed)
+    return (grid_out, grid_grad, mix_term, gain_term.reshape(CH), up_term, down_term)
 
 
 def solution(mesh):

time: 375 us -> 127 us (0.34)
  waiting for transfers between devices: 178 us -> 0 us
  blocking collectives: 76.6 us -> 0 us
  Pallas kernels: 89.9 us -> 111 us
  between operations: 14 us -> 0.65 us
  other arithmetic: 6.87 us -> 0 us
  local copies, waits for them, and re-layouts: 8.9 us -> 15.2 us
    psum x1 -> x0, waiting for transfers between devices: 178 us -> none  [local(): lax.psum((mix_term, gain_term.reshape(CH), up_term, down_term), ('lat', '...]
    psum x1 -> x0, blocking collectives: 76.6 us -> none  [local(): lax.psum((mix_term, gain_term.reshape(CH), up_term, down_term), ('lat', '...]
    pallas_call x1, Pallas kernels: 89.9 us -> 111 us  [local(): pl.pallas_call(kernel, out_shape=(jax.ShapeDtypeStruct((ROWS, COLS, CH),...]
    mul x4 -> x0, other arithmetic: 6.87 us -> none  [local(): return (grid_out, grid_grad) + tuple((term * norm_scale for term in summed))]
    unnamed x5 -> x11, local copies, waits for them, and re-layouts: 8.9 us -> 15.2 us
  transfers between devices with their start and end apart: 1 -> 0, of which waited for: 1 -> 0; matrix products, arithmetic and copies ran while one was open for 1% -> 0% of each run, Pallas kernels for 0% -> 0%
where the time goes in v2:
time: 127 us
  Pallas kernels  111 us (87%)
  local copies, waits for them, and re-layouts  15.2 us (12%)
    pallas_call x1, Pallas kernels, local(): pl.pallas_call(kernel, out_shape=(jax.ShapeDtypeStruct((ROWS, COLS, CH),...  111 us
    unnamed x11, local copies, waits for them, and re-layouts  15.2 us

profile of v2, /device:TPU:1, one launch (start us, length us, event | category | flops | bytes accessed | tf_op | source)
XLA Modules:
  0.0 127.0 jit_solution(3121261750744031147)
XLA Ops:
  0.6 1.6 %copy.20.filt = f32[4,5,1440]{2,1,0:T(8,128)} copy(f32[4,5,1440]{2,0,1:T(4,128)} %param.14) | data formatting | bytes 230400 | tf_op args[2]
  2.3 1.8 %copy.18.gin = bf16[4,180,256]{2,1,0:T(8,128)(2,1)} copy(bf16[4,180,256]{2,0,1:T(4,128)(2,1)} %param.12) | data formatting | bytes 737280 | tf_op args[0]
  4.0 1.8 %copy.19.cot = bf16[4,180,256]{2,1,0:T(8,128)(2,1)} copy(bf16[4,180,256]{2,0,1:T(4,128)(2,1)} %param.13) | data formatting | bytes 737280 | tf_op args[1]
  5.8 111.2 %shard_map.163 = (bf16[4,180,256]{2,1,0:T(8,128)(2,1)}, bf16[4,180,256]{2,1,0:T(8,128)(2,1)}, f32[256,256]{1,0:T(8,128)}, f32[1,256]{1,0:T(1,128)}, f32[256,1024]{1,0:T(8,128)}, /*index=5*/f32[1024,256]{1,0:T(8,128)}) custom-call(bf16[4,180,256]{2,1,0:T(8,128)(2,1)} %copy.18.gin, bf16[4,180,256]{2,1,0:T(8,128)(2,1)} %copy.19.cot, f32[4,5,1440]{2,1,0:T(8,128)} %copy.20.filt, ...), custom_call_target="tpu_custom_call" | custom-call | flops 4700000256 | bytes 14000000 | tf_op jit(solution)/shard_map/pallas_call | solution.py:618
  117.0 0.0 copy-start
  117.0 2.0 %copy.21 = bf16[4,180,256]{2,0,1:T(4,128)(2,1)} copy(bf16[4,180,256]{2,1,0:T(8,128)(2,1)} %get-tuple-element.18) | data formatting | bytes 737280
  118.9 1.9 %copy.22 = bf16[4,180,256]{2,0,1:T(4,128)(2,1)} copy(bf16[4,180,256]{2,1,0:T(8,128)(2,1)} %get-tuple-element.19) | data formatting | bytes 737280
  120.8 1.7 %copy.27 = f32[256,256]{1,0:T(8,128)} copy(f32[256,256]{1,0:T(8,128)} %get-tuple-element.32) | data formatting | bytes 524288
  122.5 1.2 copy.28
  123.7 2.3 %copy.29 = f32[256,1024]{1,0:T(8,128)} copy(f32[256,1024]{1,0:T(8,128)} %get-tuple-element.34) | data formatting | bytes 2097152
  126.0 0.0 copy-done
  126.0 1.0 copy.30
Async XLA Ops:
  117.0 9.0 %copy-start = (f32[1024,256]{1,0:T(8,128)S(1)}, f32[1024,256]{1,0:T(8,128)}, u32[]{:S(2)}) copy-start(f32[1024,256]{1,0:T(8,128)} %get-tuple-element.35) | copy-start | bytes 3145732

commit v3 on v1

v3 whole, which is shorter than its diff:
```python
import jax
import jax.numpy as jnp
import ml_dtypes
import numpy as np
from jax import lax
from jax.experimental import pallas as pl
from jax.experimental.pallas import tpu as pltpu
from jax.sharding import PartitionSpec as P

SQRT_TWO_PI = 0.7978845608028654
CUBIC = 0.044715
MESH = pl.DeviceIdType.MESH
BF16 = jnp.bfloat16
F32 = jnp.float32

LAT = 32
LON = 8
PAIRS = LON // 2
ROWS = 4
COLS = 180
CUT = 64
CHUNKS = 3
BLK = CUT * CHUNKS
NLON = LON * COLS
MODES = LON * BLK
WIDE = LON * CUT
CH = 256
HID = 1024
TAPS = 5
FLAT = ROWS * BLK
PART = ROWS * CUT

HALF = 2304
UP_AT, DOWN_AT = 256, 1280
GAIN_AT = 2 * HALF
PLANE = 16
SHARE = HALF // PLANE
TILE = 16
Z_ROWS = 32
NORM_SCALE = float(LAT * ROWS * NLON) ** (-0.5)


def fourier_tables():
    modes = np.arange(NLON)
    freq = np.where(modes < NLON // 2, modes, modes - NLON // 2)
    phase = (freq[:, None] * modes[None, :]) % NLON
    angle = phase * (2.0 * np.pi / NLON)
    values = np.where((modes < NLON // 2)[:, None], np.cos(angle), np.sin(angle))
    table = np.zeros((MODES, LON, BLK), np.float32)
    table[:NLON, :, :COLS] = values.reshape(NLON, LON, COLS)
    table = table.reshape(MODES, LON, CHUNKS, CUT).astype(ml_dtypes.bfloat16)
    forward = np.ascontiguousarray(table.transpose(2, 0, 1, 3)).reshape(CHUNKS, MODES, WIDE)
    inverse = np.ascontiguousarray(table.transpose(2, 1, 3, 0)).reshape(CHUNKS, WIDE, MODES)
    return forward, inverse


def expansion():
    fwd = np.zeros((32, TAPS, ROWS, 32), np.float32)
    bwd = np.zeros((64, TAPS, ROWS, 32), np.float32)
    for w in range(TAPS):
        for i in range(ROWS):
            fwd[8 * i + w, w, i] = 1.0
            bwd[8 * (i + w) + 4 - w, w, i] = 1.0
    fwd = fwd.reshape(32, TAPS * 128)
    bwd = bwd.reshape(64, TAPS * 128)
    return fwd.astype(ml_dtypes.bfloat16), bwd.astype(ml_dtypes.bfloat16)


def dot(a, b):
    return jnp.dot(a, b, preferred_element_type=F32)


def dot_rows(a, b):
    return lax.dot_general(a, b, (((0,), (0,)), ((), ())), preferred_element_type=F32)


def dot_transpose(a, b):
    return lax.dot_general(a, b, (((1,), (1,)), ((), ())), preferred_element_type=F32)


def lanes_of(shape):
    return lax.broadcasted_iota(jnp.int32, shape, 1)


def turn_groups(parts):
    lane = lanes_of(parts[0].shape)
    low = lane < 64
    a, b, c, d = parts
    a, c = jnp.where(low, a, pltpu.roll(c, 64, 1)), jnp.where(low, pltpu.roll(a, 64, 1), c)
    b, d = jnp.where(low, b, pltpu.roll(d, 64, 1)), jnp.where(low, pltpu.roll(b, 64, 1), d)
    even = (lane % 64) < 32
    a, b = jnp.where(even, a, pltpu.roll(b, 32, 1)), jnp.where(even, pltpu.roll(a, 96, 1), b)
    c, d = jnp.where(even, c, pltpu.roll(d, 32, 1)), jnp.where(even, pltpu.roll(c, 96, 1), d)
    return a, b, c, d


def kernel(
    gin_hbm, cot_hbm, filt_hbm, band, wmix_hbm, gain_hbm, wup_hbm, wdown_hbm, efwd_hbm, ebwd_hbm, fwd_hbm, inv_hbm,
    out, grad, sums,
    fwd, inv, gf, cflat, send, recv, hsend, hrecv, halo, fstage, fown, fhalo, coef, dcoef,
    spec, banded, cf, conv, field, stream, scaled, before, dhid, hidden, dbef, ds, ds16, res, gres,
    gsum, part, csend, crecv, ps, pr, zf, zs, zr, zall, fin,
    gin, cot, filt, wmix, gain, wup, wdown, efwd, ebwd,
    isem, osem, ssem, rsem, hssem, hrsem, fssem, frsem, cssem, crsem, pssem, prsem, zssem, zrsem,
):
    lat = lax.axis_index("lat")
    me = lax.axis_index("lon")
    pair = me // 2
    after = lax.rem(lat + 1, LAT)
    ahead = lax.rem(lat + LAT - 1, LAT)
    core = me - 2 * pair
    x = lat // 8
    z_lo = lat // 4 - 2 * x
    y = lat - 8 * x - 4 * z_lo
    z = 2 * pair + z_lo
    mine = pl.multiple_of(core * HALF, HALF)

    plane = 4 * x + y

    def plane_peer(to):
        return {"lat": to // 4 * 8 + z_lo * 4 + (to - to // 4 * 4)}

    def z_peer(to):
        return {"lat": x * 8 + (to - to // 2 * 2) * 4 + y, "lon": to // 2 * 2 + core}

    inputs = (
        (gin_hbm, gin), (filt_hbm, filt), (efwd_hbm, efwd), (cot_hbm, cot), (wdown_hbm, wdown), (fwd_hbm, fwd),
        (inv_hbm, inv), (ebwd_hbm, ebwd), (wmix_hbm, wmix), (gain_hbm, gain), (wup_hbm, wup),
    )
    gets = [pltpu.make_async_copy(src, dst, isem.at[k]) for k, (src, dst) in enumerate(inputs)]
    gets[0].start()

    barrier = pltpu.get_barrier_semaphore()
    for s in range(1, LON):
        pl.semaphore_signal(barrier, inc=1, device_id={"lon": lax.rem(me + s, LON)}, device_id_type=MESH)
    for there in (after, ahead):
        pl.semaphore_signal(barrier, inc=1, device_id={"lat": there}, device_id_type=MESH)
    for s in range(1, PLANE):
        there = plane_peer(lax.rem(plane + s, PLANE))
        pl.semaphore_signal(barrier, inc=1, device_id=there, device_id_type=MESH)
    for s in range(1, 8):
        pl.semaphore_signal(barrier, inc=1, device_id=z_peer(lax.rem(z + s, 8)), device_id_type=MESH)

    for get in gets[1:]:
        get.start()

    def exchange(ph, c, to, own):
        return pltpu.make_async_remote_copy(
            src_ref=send.at[ph, c, to], dst_ref=recv.at[ph, c, own],
            send_sem=ssem.at[ph, c, to], recv_sem=rsem.at[ph, c, own],
            device_id={"lon": to}, device_id_type=MESH,
        )

    def start_exchange(ph, c):
        for s in (4, 3, 5, 2, 6, 7, 1):
            exchange(ph, c, lax.rem(me + s, LON), me).start()
        recv[ph, c, me] = send[ph, c, me]

    def arrived(ph, c):
        for s in range(1, LON):
            there = lax.rem(me + s, LON)
            exchange(ph, c, there, there).wait_recv()

    def halo_copy(hp, side, c):
        return pltpu.make_async_remote_copy(
            src_ref=hsend.at[hp, side, c], dst_ref=hrecv.at[hp, side, c],
            send_sem=hssem.at[hp, side, c], recv_sem=hrsem.at[hp, side, c],
            device_id={"lat": after if side == 0 else ahead}, device_id_type=MESH,
        )

    def filter_copy(side):
        return pltpu.make_async_remote_copy(
            src_ref=fown.at[pl.ds(16 if side == 0 else 0, 16)], dst_ref=fhalo.at[side],
            send_sem=fssem.at[side], recv_sem=frsem.at[side],
            device_id={"lat": after if side == 0 else ahead}, device_id_type=MESH,
        )

    def pack(src, ph, c):
        for half in range(2):
            parts = [src[half, pl.ds(c * PART + i, CUT, stride=ROWS), :] for i in range(ROWS)]
            for g, block in enumerate(turn_groups(parts)):
                send[ph, c, half * 4 + g] = block.astype(BF16)

    def unpack(ph, c, put):
        for half in range(2):
            parts = [recv[ph, c, half * 4 + g].astype(F32) for g in range(4)]
            for i, block in enumerate(turn_groups(parts)):
                put(half, pl.ds(c * PART + i, CUT, stride=ROWS), block)

    def pass_halo(ph, hp, c):
        arrived(ph, c)
        for g in range(PAIRS):
            one = recv[ph, c, 2 * g].astype(F32)
            two = recv[ph, c, 2 * g + 1].astype(F32)
            low = lanes_of(one.shape) < 64
            hsend[hp, 0, c, g] = jnp.where(low, pltpu.roll(one, 64, 1), two).astype(BF16)
            hsend[hp, 1, c, g] = jnp.where(low, one, pltpu.roll(two, 64, 1)).astype(BF16)
        halo_copy(hp, 0, c).start()
        halo_copy(hp, 1, c).start()

    def to_modes(ph, hp, c):
        halo_copy(hp, 0, c).wait_recv()
        halo_copy(hp, 1, c).wait_recv()
        for g in range(PAIRS):
            one = hrecv[hp, 0, c, g].astype(F32)
            two = hrecv[hp, 1, c, g].astype(F32)
            low = lanes_of(one.shape) < 64
            halo[c, 2 * g] = jnp.where(low, one, pltpu.roll(two, 64, 1)).astype(BF16)
            halo[c, 2 * g + 1] = jnp.where(low, pltpu.roll(one, 64, 1), two).astype(BF16)

        @pl.loop(0, MODES // 512)
        def _(step):
            at = pl.ds(pl.multiple_of(step * 512, 512), 512)
            both = jnp.concatenate(
                [recv[ph, c].reshape(WIDE, 128), halo[c].reshape(WIDE, 128)], axis=1
            )
            term = dot(fwd[c, at, :], both)
            spec[at, :] = term if c == 0 else spec[at, :] + term

    def band_sum(weights, first, last):
        @pl.loop(first, last)
        def _(step):
            at = pl.ds(pl.multiple_of(step * 128, 128), 128)
            own = spec[at, 0:128]
            edge = spec[at, 128:256]
            lane = lanes_of(own.shape)
            half = pltpu.roll(own, 64, 1)
            windows = (
                jnp.where(lane < 64, edge, half),
                jnp.where(lane < 32, pltpu.roll(edge, 96, 1), pltpu.roll(own, 32, 1)),
                own,
                jnp.where(lane >= 96, pltpu.roll(edge, 32, 1), pltpu.roll(own, 96, 1)),
                jnp.where(lane >= 64, edge, half),
            )
            total = windows[0] * weights[at, 0:128]
            for w in range(1, TAPS):
                total = total + windows[w] * weights[at, w * 128 : w * 128 + 128]
            banded[at, :] = total.astype(BF16)

    def to_grid(ph, c):
        block = dot(inv[c], banded[...]).astype(BF16)
        for q in range(LON):
            send[ph, c, q] = block[q * CUT : q * CUT + CUT]
        start_exchange(ph, c)

    theirs = pl.multiple_of((1 - core) * HALF, HALF)
    other_core = {"lon": me + 1 - 2 * core}
    gain_rows = pl.ds(GAIN_AT, TILE)

    def core_copy(kind):
        rows = pl.ds(0, DOWN_AT) if kind == 0 else pl.ds(DOWN_AT, HALF + TILE - DOWN_AT)
        return pltpu.make_async_remote_copy(
            src_ref=csend.at[rows], dst_ref=crecv.at[rows], send_sem=cssem.at[kind], recv_sem=crsem.at[kind],
            device_id=other_core, device_id_type=MESH,
        )

    def core_gather(base, k):
        rows = pl.ds(base + k * SHARE, SHARE)
        return pltpu.make_async_remote_copy(
            src_ref=fin.at[rows], dst_ref=fin.at[rows], send_sem=cssem.at[2 + k], recv_sem=crsem.at[2 + k],
            device_id=other_core, device_id_type=MESH,
        )

    def plane_copy(kind, to, own):
        src, dst = (
            (ps.at[to], pr.at[own]),
            (zall.at[pl.ds(0, SHARE)], fin.at[pl.ds(mine + own * SHARE, SHARE)]),
        )[kind]
        return src, dst

    def z_copy(kind, to, own):
        src, dst = (
            (zs.at[pl.ds(to * Z_ROWS, Z_ROWS)], zr.at[own]),
            (zall.at[pl.ds(own * Z_ROWS, Z_ROWS)], zall.at[pl.ds(own * Z_ROWS, Z_ROWS)]),
        )[kind]
        return src, dst

    rings = {
        "plane": (plane, PLANE, plane_copy, plane_peer, pssem, prsem),
        "z": (z, 8, z_copy, z_peer, zssem, zrsem),
    }

    def ring_copy(axis, kind, to, own):
        _, _, copy, peer, send_sems, recv_sems = rings[axis]
        src, dst = copy(kind, to, own)
        return pltpu.make_async_remote_copy(
            src_ref=src, dst_ref=dst, send_sem=send_sems.at[kind, to], recv_sem=recv_sems.at[kind, own],
            device_id=peer(to), device_id_type=MESH,
        )

    def ring_start(axis, kind):
        here, count = rings[axis][:2]
        for s in range(1, count):
            ring_copy(axis, kind, lax.rem(here + s, count), here).start()

    def ring_arrived(axis, kind):
        here, count = rings[axis][:2]
        for s in range(1, count):
            there = lax.rem(here + s, count)
            ring_copy(axis, kind, there, there).wait_recv()

    def ring_sent(axis, kind):
        here, count = rings[axis][:2]
        for s in range(1, count):
            ring_copy(axis, kind, lax.rem(here + s, count), here).wait_send()

    def others(ref, here, count, rows):
        total = ref[lax.rem(here + 1, count), rows, :].astype(F32)
        for s in range(2, count):
            total = total + ref[lax.rem(here + s, count), rows, :].astype(F32)
        return total

    def send_half(first, last):
        @pl.loop(first // 256, last // 256)
        def _(step):
            csend[pl.ds(step * 256, 256), :] = part[pl.ds(theirs + step * 256, 256), :].astype(BF16)

    def scatter_plane():
        core_copy(0).wait_recv()
        core_copy(1).wait_recv()
        g = part[gain_rows, :] + crecv[HALF:, :].astype(F32)
        part[gain_rows, :] = g

        @pl.loop(0, PLANE)
        def _(to):
            v = part[pl.ds(mine + to * SHARE, SHARE), :] + crecv[pl.ds(to * SHARE, SHARE), :].astype(F32)
            part[pl.ds(mine + to * SHARE, SHARE), :] = v
            ps[to, 0:SHARE, :] = v.astype(BF16)
            ps[to, SHARE:, :] = g.astype(BF16)

        ring_start("plane", 0)

    def scatter_z():
        ring_arrived("plane", 0)
        zf[SHARE + TILE :, :] = jnp.zeros((8 * Z_ROWS - SHARE - TILE, 128), F32)
        zf[0:SHARE, :] = part[pl.ds(mine + plane * SHARE, SHARE), :] + others(pr, plane, PLANE, pl.ds(0, SHARE))
        zf[SHARE : SHARE + TILE, :] = part[gain_rows, :] + others(pr, plane, PLANE, pl.ds(SHARE, TILE))
        zs[...] = zf[...].astype(BF16)
        ring_start("z", 0)

    def gather_z():
        ring_arrived("z", 0)
        rows = pl.ds(pl.multiple_of(z * Z_ROWS, Z_ROWS), Z_ROWS)
        zall[rows, :] = (zf[rows, :] + others(zr, z, 8, pl.ds(0, Z_ROWS))).astype(BF16)
        ring_start("z", 1)

    def gather_plane():
        ring_arrived("z", 1)
        ring_start("plane", 1)
        fin[pl.ds(mine + plane * SHARE, SHARE), :] = zall[0:SHARE, :]
        core_gather(mine, plane).start()

    def gather_core():
        for s in range(1, PLANE):
            there = lax.rem(plane + s, PLANE)
            ring_copy("plane", 1, there, there).wait_recv()
            core_gather(mine, there).start()

    gets[0].wait()
    for half in range(2):
        gf[half, ROWS * COLS :, :] = jnp.zeros((FLAT - ROWS * COLS, 128), F32)
    for c in range(CHUNKS):
        count = min(CUT, COLS - c * CUT)
        rows = gin[c * CUT : c * CUT + count].astype(F32).reshape(ROWS * count, CH)
        for half in range(2):
            gf[half, c * PART : c * PART + ROWS * count, :] = rows[:, half * 128 : half * 128 + 128]
    pack(gf, 0, 0)
    pl.semaphore_wait(barrier, LON - 1 + 2 + PLANE - 1 + 7)
    start_exchange(0, 0)
    for c in range(1, CHUNKS):
        pack(gf, 0, c)
        start_exchange(0, c)

    gets[1].wait()
    gets[2].wait()
    fstage[...] = jnp.zeros_like(fstage)
    row = lax.broadcasted_iota(jnp.int32, (ROWS, NLON), 0)
    mode = lax.broadcasted_iota(jnp.int32, (ROWS, NLON), 1)
    scale = jnp.where(mode == 0, 1.0 / NLON, 2.0 / NLON)
    reach = jnp.where(row == 0, band[0], jnp.where(row == 1, band[1], jnp.where(row == 2, band[2], band[3])))
    for t in range(TAPS):
        at = lat * ROWS + row + (t - 2)
        keep = (reach >= abs(t - 2)) & (at >= 0) & (at < LAT * ROWS)
        kept = jnp.where(keep, filt[t] * scale, 0.0)
        for i in range(ROWS):
            fstage[8 * i + t : 8 * i + t + 1, 0:NLON] = kept[i : i + 1, :]
    fown[...] = fstage[...].astype(BF16)
    filter_copy(0).start()
    filter_copy(1).start()

    @pl.loop(0, MODES // 256)
    def _(step):
        at = pl.ds(pl.multiple_of(step * 256, 256), 256)
        coef[at, :] = dot_rows(fown[:, at], efwd[...])

    gets[3].wait()
    gets[4].wait()
    cflat[ROWS * COLS :, :] = jnp.zeros((FLAT - ROWS * COLS, CH), BF16)
    cflat[0 : ROWS * COLS, :] = cot[...].reshape(ROWS * COLS, CH)
    dhid[...] = dot_transpose(cflat[...], wdown[...])
    gsum[...] = jnp.zeros_like(gsum)

    for c in range(CHUNKS):
        pass_halo(0, 0, c)
    gets[5].wait()
    for c in range(CHUNKS):
        to_modes(0, 0, c)
    band_sum(coef, 0, MODES // 128)
    gets[6].wait()
    for c in range(CHUNKS):
        to_grid(1, c)

    for get in gets[7:]:
        get.wait()
    filter_copy(0).wait()
    filter_copy(1).wait()

    @pl.loop(0, MODES // 256)
    def _(step):
        at = pl.ds(pl.multiple_of(step * 256, 256), 256)
        rows = jnp.concatenate([fhalo[0, :, at], fown[:, at], fhalo[1, :, at]], axis=0)
        dcoef[at, :] = dot_rows(rows, ebwd[...])

    def put_conv(half, rows, block):
        cf[half, rows, :] = block

    def tail(c):
        arrived(1, c)
        unpack(1, c, put_conv)
        all_rows = pl.ds(c * PART, PART)
        conv[all_rows, :] = jnp.concatenate([cf[0, all_rows, :], cf[1, all_rows, :]], axis=1).astype(BF16)
        field[all_rows, :] = dot(conv[all_rows, :], wmix[...])

        @pl.loop(0, PART // 128)
        def _(step):
            at = pl.ds(c * PART + step * 128, 128)
            mixed = field[at, :] + jnp.concatenate([gf[0, at, :], gf[1, at, :]], axis=1)
            s16 = mixed.astype(BF16)
            stream[at, :] = s16
            sf = s16.astype(F32)
            inverse = lax.rsqrt(jnp.mean(sf * sf, axis=-1, keepdims=True) + 1e-06)
            scaled[at, :] = (sf * inverse * gain[...]).astype(BF16)

        before[all_rows, :] = dot(scaled[all_rows, :], wup[...])

        @pl.loop(0, PART // 16)
        def _(step):
            at = pl.ds(c * PART + step * 16, 16)
            u = before[at, :]
            u2 = u * u
            tangent = jnp.tanh(u * (SQRT_TWO_PI + (SQRT_TWO_PI * CUBIC) * u2))
            h = 0.5 * u
            hidden[at, :] = (h + h * tangent).astype(BF16)
            slope = (0.5 + 0.5 * tangent) + (h * (1.0 - tangent * tangent)) * (
                SQRT_TWO_PI + (3.0 * SQRT_TWO_PI * CUBIC) * u2
            )
            dbef[at, :] = (dhid[at, :] * slope).astype(BF16)

        field[all_rows, :] = dot_transpose(dbef[all_rows, :], wup[...])

        @pl.loop(0, PART // 128)
        def _(step):
            at = pl.ds(c * PART + step * 128, 128)
            sf = stream[at, :].astype(F32)
            inverse = lax.rsqrt(jnp.mean(sf * sf, axis=-1, keepdims=True) + 1e-06)
            normed = sf * inverse
            d_scaled = field[at, :]
            gsum[...] += jnp.sum(d_scaled * normed, axis=0, keepdims=True)
            gained = d_scaled * gain[...]
            value = cflat[at, :].astype(F32) + inverse * (
                gained - normed * jnp.mean(gained * normed, axis=-1, keepdims=True)
            )
            for half in range(2):
                ds[half, at, :] = value[:, half * 128 : half * 128 + 128]
            ds16[at, :] = value.astype(BF16)

        d_conv = dot_transpose(ds16[all_rows, :], wmix[...])
        for half in range(2):
            cf[half, all_rows, :] = d_conv[:, half * 128 : half * 128 + 128]
        pack(cf, 2, c)
        start_exchange(2, c)

    for c in range(CHUNKS):
        tail(c)

    term = dot_rows(conv[...], ds16[...])
    for h in range(2):
        part[h * HALF : h * HALF + UP_AT, :] = term[:, h * 128 : h * 128 + 128]
    term = dot_rows(scaled[...], dbef[...])
    for h in range(8):
        at = h // 4 * HALF + UP_AT + h % 4 * 256
        part[at : at + 256, :] = term[:, h * 128 : h * 128 + 128]
    send_half(0, DOWN_AT)
    core_copy(0).start()
    term = dot_rows(hidden[...], cflat[...])
    for h in range(2):
        part[h * HALF + DOWN_AT : (h + 1) * HALF, :] = term[:, h * 128 : h * 128 + 128]
    part[gain_rows, :] = jnp.zeros((TILE, 128), F32)
    for h in range(2):
        part[GAIN_AT + h : GAIN_AT + h + 1, :] = gsum[:, h * 128 : h * 128 + 128]
    send_half(DOWN_AT, HALF)
    csend[HALF:, :] = part[gain_rows, :].astype(BF16)
    core_copy(1).start()

    result = stream[...].astype(F32) + dot(hidden[...], wdown[...])
    res[...] = result[0 : ROWS * COLS].reshape(COLS, ROWS, CH).astype(BF16)
    put_out = pltpu.make_async_copy(res, out, osem.at[0])
    put_out.start()
    scatter_plane()

    for c in range(CHUNKS):
        pass_halo(2, 1, c)
    for c in range(CHUNKS):
        to_modes(2, 1, c)
    scatter_z()
    band_sum(dcoef, 0, MODES // 128)
    for c in range(CHUNKS):
        to_grid(3, c)
    gather_z()

    def put_grad(half, rows, block):
        ds[half, rows, :] = block + ds[half, rows, :]

    gather_plane()
    for c in range(CHUNKS):
        arrived(3, c)
        unpack(3, c, put_grad)
        count = min(CUT, COLS - c * CUT)
        rows = pl.ds(c * PART, ROWS * count)
        both = jnp.concatenate([ds[0, rows, :], ds[1, rows, :]], axis=1)
        gres[c * CUT : c * CUT + count] = both.reshape(count, ROWS, CH).astype(BF16)
    put_grad_out = pltpu.make_async_copy(gres, grad, osem.at[1])
    put_grad_out.start()
    gather_core()
    put_gain = pltpu.make_async_copy(zall.at[pl.ds(SHARE, TILE)], sums.at[pl.ds(GAIN_AT, TILE)], osem.at[2])
    put_own = pltpu.make_async_copy(fin.at[pl.ds(mine, HALF)], sums.at[pl.ds(mine, HALF)], osem.at[3])
    put_other = pltpu.make_async_copy(fin.at[pl.ds(theirs, HALF)], sums.at[pl.ds(theirs, HALF)], osem.at[4])
    put_gain.start()
    put_own.start()
    for k in range(PLANE):
        core_gather(theirs, k).wait_recv()
    put_other.start()

    core_copy(0).wait_send()
    core_copy(1).wait_send()
    for k in range(PLANE):
        core_gather(mine, k).wait_send()
    for kind in range(2):
        ring_sent("plane", kind)
        ring_sent("z", kind)
    for ph in range(4):
        for c in range(CHUNKS):
            for s in range(1, LON):
                exchange(ph, c, lax.rem(me + s, LON), me).wait_send()
    for hp in range(2):
        for c in range(CHUNKS):
            halo_copy(hp, 0, c).wait_send()
            halo_copy(hp, 1, c).wait_send()
    put_out.wait()
    put_grad_out.wait()
    put_gain.wait()
    put_own.wait()
    put_other.wait()


def finish(res, gres, sums, out, grad, mix_o, gain_o, up_o, down_o):
    out[...] = res[...]
    grad[...] = gres[...]
    for h in range(2):
        lanes = slice(h * 128, h * 128 + 128)
        at = h * HALF
        mix_o[:, lanes] = sums[at : at + UP_AT, :].astype(F32) * NORM_SCALE
        down_o[:, lanes] = sums[at + DOWN_AT : at + HALF, :].astype(F32) * NORM_SCALE
        gain_o[:, lanes] = sums[GAIN_AT : GAIN_AT + TILE, :].astype(F32)[h : h + 1, :] * NORM_SCALE
    for h in range(8):
        at = h // 4 * HALF + UP_AT + h % 4 * 256
        up_o[:, h * 128 : h * 128 + 128] = sums[at : at + 256, :].astype(F32) * NORM_SCALE


def local(grid_in, grid_cotangent, support_filter, band_half, w_mix, norm_gain, w_up, w_down):
    forward, inverse = fourier_tables()
    efwd, ebwd = expansion()
    vmem = pl.BlockSpec(memory_space=pltpu.VMEM)
    smem = pl.BlockSpec(memory_space=pltpu.SMEM)
    anywhere = pl.BlockSpec(memory_space=pl.ANY)
    field = jax.ShapeDtypeStruct((COLS, ROWS, CH), BF16)
    res, gres, sums = pl.pallas_call(
        kernel,
        out_shape=(field, field, jax.ShapeDtypeStruct((2 * HALF + TILE, 128), BF16)),
        in_specs=[anywhere] * 3 + [smem] + [anywhere] * 8,
        out_specs=[anywhere] * 3,
        scratch_shapes=[
            pltpu.VMEM((CHUNKS, MODES, WIDE), BF16),
            pltpu.VMEM((CHUNKS, WIDE, MODES), BF16),
            pltpu.VMEM((2, FLAT, 128), F32),
            pltpu.VMEM((FLAT, CH), BF16),
            pltpu.VMEM((4, CHUNKS, LON, CUT, 128), BF16),
            pltpu.VMEM((4, CHUNKS, LON, CUT, 128), BF16),
            pltpu.VMEM((2, 2, CHUNKS, PAIRS, CUT, 128), BF16),
            pltpu.VMEM((2, 2, CHUNKS, PAIRS, CUT, 128), BF16),
            pltpu.VMEM((CHUNKS, LON, CUT, 128), BF16),
            pltpu.VMEM((32, MODES), F32),
            pltpu.VMEM((32, MODES), BF16),
            pltpu.VMEM((2, 16, MODES), BF16),
            pltpu.VMEM((MODES, TAPS * 128), F32),
            pltpu.VMEM((MODES, TAPS * 128), F32),
            pltpu.VMEM((MODES, 256), F32),
            pltpu.VMEM((MODES, 128), BF16),
            pltpu.VMEM((2, FLAT, 128), F32),
            pltpu.VMEM((FLAT, CH), BF16),
            pltpu.VMEM((FLAT, CH), F32),
            pltpu.VMEM((FLAT, CH), BF16),
            pltpu.VMEM((FLAT, CH), BF16),
            pltpu.VMEM((FLAT, HID), F32),
            pltpu.VMEM((FLAT, HID), F32),
            pltpu.VMEM((FLAT, HID), BF16),
            pltpu.VMEM((FLAT, HID), BF16),
            pltpu.VMEM((2, FLAT, 128), F32),
            pltpu.VMEM((FLAT, CH), BF16),
            pltpu.VMEM((COLS, ROWS, CH), BF16),
            pltpu.VMEM((COLS, ROWS, CH), BF16),
            pltpu.VMEM((1, CH), F32),
            pltpu.VMEM((2 * HALF + TILE, 128), F32),
            pltpu.VMEM((HALF + TILE, 128), BF16),
            pltpu.VMEM((HALF + TILE, 128), BF16),
            pltpu.VMEM((PLANE, SHARE + TILE, 128), BF16),
            pltpu.VMEM((PLANE, SHARE + TILE, 128), BF16),
            pltpu.VMEM((8 * Z_ROWS, 128), F32),
            pltpu.VMEM((8 * Z_ROWS, 128), BF16),
            pltpu.VMEM((8, Z_ROWS, 128), BF16),
            pltpu.VMEM((8 * Z_ROWS, 128), BF16),
            pltpu.VMEM((2 * HALF, 128), BF16),
            pltpu.VMEM((COLS, ROWS, CH), BF16),
            pltpu.VMEM((COLS, ROWS, CH), BF16),
            pltpu.VMEM((TAPS, ROWS, NLON), F32),
            pltpu.VMEM((CH, CH), BF16),
            pltpu.VMEM((1, CH), F32),
            pltpu.VMEM((CH, HID), BF16),
            pltpu.VMEM((HID, CH), BF16),
            pltpu.VMEM((32, TAPS * 128), BF16),
            pltpu.VMEM((64, TAPS * 128), BF16),
            pltpu.SemaphoreType.DMA((11,)),
            pltpu.SemaphoreType.DMA((5,)),
            pltpu.SemaphoreType.DMA((4, CHUNKS, LON)),
            pltpu.SemaphoreType.DMA((4, CHUNKS, LON)),
            pltpu.SemaphoreType.DMA((2, 2, CHUNKS)),
            pltpu.SemaphoreType.DMA((2, 2, CHUNKS)),
            pltpu.SemaphoreType.DMA((2,)),
            pltpu.SemaphoreType.DMA((2,)),
            pltpu.SemaphoreType.DMA((2 + PLANE,)),
            pltpu.SemaphoreType.DMA((2 + PLANE,)),
            pltpu.SemaphoreType.DMA((2, PLANE)),
            pltpu.SemaphoreType.DMA((2, PLANE)),
            pltpu.SemaphoreType.DMA((2, 8)),
            pltpu.SemaphoreType.DMA((2, 8)),
        ],
        compiler_params=pltpu.CompilerParams(
            collective_id=0, has_side_effects=True, vmem_limit_bytes=60 * 1024 * 1024
        ),
        cost_estimate=pl.CostEstimate(flops=4_700_000_000, bytes_accessed=14_000_000, transcendentals=800_000),
    )(
        jnp.transpose(grid_in, (1, 0, 2)), jnp.transpose(grid_cotangent, (1, 0, 2)),
        jnp.transpose(support_filter, (1, 0, 2)), band_half, w_mix, norm_gain.reshape(1, CH), w_up, w_down,
        jnp.asarray(efwd), jnp.asarray(ebwd), jnp.asarray(forward), jnp.asarray(inverse),
    )
    grid_out, grid_grad, mix_grad, gain_grad, up_grad, down_grad = pl.pallas_call(
        finish,
        out_shape=(
            field,
            field,
            jax.ShapeDtypeStruct((CH, CH), F32),
            jax.ShapeDtypeStruct((1, CH), F32),
            jax.ShapeDtypeStruct((CH, HID), F32),
            jax.ShapeDtypeStruct((HID, CH), F32),
        ),
        in_specs=[vmem] * 3,
        out_specs=[vmem] * 6,
        compiler_params=pltpu.CompilerParams(vmem_limit_bytes=60 * 1024 * 1024),
    )(res, gres, sums)
    return (
        jnp.transpose(grid_out, (1, 0, 2)),
        jnp.transpose(grid_grad, (1, 0, 2)),
        mix_grad,
        gain_grad.reshape(CH),
        up_grad,
        down_grad,
    )


def solution(mesh):
    return jax.shard_map(
        local,
        mesh=mesh,
        in_specs=(
            P("lat", "lon", None),
            P("lat", "lon", None),
            P("lat", None, None),
            P("lat"),
            P(),
            P(),
            P(),
            P(),
        ),
        out_specs=(P("lat", "lon", None), P("lat", "lon", None), P(), P(), P(), P()),
        check_vma=False,
    )
```

time: 375 us -> 102 us (0.27)
  waiting for transfers between devices: 178 us -> 0 us
  blocking collectives: 76.6 us -> 0 us
  between operations: 14 us -> 0.64 us
  Pallas kernels: 89.9 us -> 101 us
  local copies, waits for them, and re-layouts: 8.9 us -> 0 us
  other arithmetic: 6.87 us -> 0 us
    psum x1 -> x0, waiting for transfers between devices: 178 us -> none  [local(): lax.psum((mix_term, gain_term.reshape(CH), up_term, down_term), ('lat', '...]
    psum x1 -> x0, blocking collectives: 76.6 us -> none  [local(): lax.psum((mix_term, gain_term.reshape(CH), up_term, down_term), ('lat', '...]
    pallas_call x1 -> x2, Pallas kernels: 89.9 us -> 101 us  [the longest x1 97.8 us: local(): pl.pallas_call(kernel, out_shape=(field, field, jax.ShapeDtypeStruct((2 *...]
    unnamed x5 -> x0, local copies, waits for them, and re-layouts: 8.9 us -> none
    mul x4 -> x0, other arithmetic: 6.87 us -> none  [local(): return (grid_out, grid_grad) + tuple((term * norm_scale for term in summed))]
  transfers between devices with their start and end apart: 1 -> 0, of which waited for: 1 -> 0; matrix products, arithmetic and copies ran while one was open for 1% -> 0% of each run, Pallas kernels for 0% -> 0%
where the time goes in v3:
time: 102 us
  Pallas kernels  101 us (99%)
    pallas_call x1, Pallas kernels, local(): pl.pallas_call(kernel, out_shape=(field, field, jax.ShapeDtypeStruct((2 *...  97.8 us
    pallas_call x1, Pallas kernels, local(): pl.pallas_call(finish, out_shape=(field, field, jax.ShapeDtypeStruct((CH,...  3.21 us

profile of v3, /device:TPU:1, one launch (start us, length us, event | category | flops | bytes accessed | tf_op | source)
XLA Modules:
  0.0 101.6 jit_solution(5763001704145601204)
XLA Ops:
  0.6 97.8 %shard_map.163 = (bf16[180,4,256]{2,1,0:T(4,128)(2,1)}, bf16[180,4,256]{2,1,0:T(4,128)(2,1)}, bf16[4624,128]{1,0:T(8,128)(2,1)}) custom-call(bf16[180,4,256]{2,1,0:T(4,128)(2,1)} %bitcast.7, bf16[180,4,256]{2,1,0:T(4,128)(2,1)} %bitcast.8, f32[5,4,1440]{2,1,0:T(4,128)} %bitcast.11, s32[4]{0:T(128)} %band.1, bf16[256,256]{1,0:T(8,128)(2,1)} %wmix_hbm.1, ...), custom_call_target="tpu_custom_call" | custom-call | flops 4700000256 | bytes 14000000 | tf_op jit(solution)/shard_map/pallas_call | solution.py:587
  98.4 3.2 %shard_map.164 = (bf16[180,4,256]{2,1,0:T(4,128)(2,1)}, bf16[180,4,256]{2,1,0:T(4,128)(2,1)}, f32[256,256]{1,0:T(8,128)}, f32[1,256]{1,0:T(1,128)}, f32[256,1024]{1,0:T(8,128)}, /*index=5*/f32[1024,256]{1,0:T(8,128)}) custom-call(bf16[180,4,256]{2,1,0:T(4,128)(2,1)} %get-tuple-element.15.res, bf16[180,4,256]{2,1,0:T(4,128)(2,1)} %get-tuple-element.16.gres, ...), custom_call_target="tpu_custom_call" | custom-call | tf_op jit(solution)/shard_map/pallas_call | solution.py:666

commit v4 on v3

--- a/solution.py
+++ b/solution.py
@@ -35,6 +35,7 @@
 GAIN_AT = 2 * HALF
 PLANE = 16
 SHARE = HALF // PLANE
+GROUP = 5
 TILE = 16
 Z_ROWS = 32
 NORM_SCALE = float(LAT * ROWS * NLON) ** (-0.5)
@@ -95,12 +96,12 @@
 
 
 def kernel(
-    gin_hbm, cot_hbm, filt_hbm, band, wmix_hbm, gain_hbm, wup_hbm, wdown_hbm, efwd_hbm, ebwd_hbm, fwd_hbm, inv_hbm,
+    gin_hbm, cot_hbm, filt_hbm, band_hbm, wmix_hbm, gain_hbm, wup_hbm, wdown_hbm, efwd_hbm, ebwd_hbm, fwd_hbm, inv_hbm,
     out, grad, sums,
     fwd, inv, gf, cflat, send, recv, hsend, hrecv, halo, fstage, fown, fhalo, coef, dcoef,
     spec, banded, cf, conv, field, stream, scaled, before, dhid, hidden, dbef, ds, ds16, res, gres,
     gsum, part, csend, crecv, ps, pr, zf, zs, zr, zall, fin,
-    gin, cot, filt, wmix, gain, wup, wdown, efwd, ebwd,
+    gin, cot, filt, band, wmix, gain, wup, wdown, efwd, ebwd,
     isem, osem, ssem, rsem, hssem, hrsem, fssem, frsem, cssem, crsem, pssem, prsem, zssem, zrsem,
 ):
     lat = lax.axis_index("lat")
@@ -125,7 +126,7 @@
 
     inputs = (
         (gin_hbm, gin), (filt_hbm, filt), (efwd_hbm, efwd), (cot_hbm, cot), (wdown_hbm, wdown), (fwd_hbm, fwd),
-        (inv_hbm, inv), (ebwd_hbm, ebwd), (wmix_hbm, wmix), (gain_hbm, gain), (wup_hbm, wup),
+        (inv_hbm, inv), (ebwd_hbm, ebwd), (wmix_hbm, wmix), (gain_hbm, gain), (wup_hbm, wup), (band_hbm, band),
     )
     gets = [pltpu.make_async_copy(src, dst, isem.at[k]) for k, (src, dst) in enumerate(inputs)]
     gets[0].start()
@@ -147,7 +148,7 @@
     def exchange(ph, c, to, own):
         return pltpu.make_async_remote_copy(
             src_ref=send.at[ph, c, to], dst_ref=recv.at[ph, c, own],
-            send_sem=ssem.at[ph, c, to], recv_sem=rsem.at[ph, c, own],
+            send_sem=ssem.at[ph], recv_sem=rsem.at[ph, c],
             device_id={"lon": to}, device_id_type=MESH,
         )
 
@@ -156,22 +157,26 @@
             exchange(ph, c, lax.rem(me + s, LON), me).start()
         recv[ph, c, me] = send[ph, c, me]
 
+    def all_of(ref, sem):
+        return pltpu.make_async_remote_copy(
+            src_ref=ref, dst_ref=ref, send_sem=sem, recv_sem=sem,
+            device_id={"lon": lax.rem(me + 1, LON)}, device_id_type=MESH,
+        )
+
     def arrived(ph, c):
-        for s in range(1, LON):
-            there = lax.rem(me + s, LON)
-            exchange(ph, c, there, there).wait_recv()
+        all_of(recv.at[ph, c, pl.ds(0, LON - 1)], rsem.at[ph, c]).wait_recv()
 
     def halo_copy(hp, side, c):
         return pltpu.make_async_remote_copy(
-            src_ref=hsend.at[hp, side, c], dst_ref=hrecv.at[hp, side, c],
-            send_sem=hssem.at[hp, side, c], recv_sem=hrsem.at[hp, side, c],
+            src_ref=hsend.at[hp, c, side], dst_ref=hrecv.at[hp, c, side],
+            send_sem=hssem.at[hp], recv_sem=hrsem.at[hp, c],
             device_id={"lat": after if side == 0 else ahead}, device_id_type=MESH,
         )
 
     def filter_copy(side):
         return pltpu.make_async_remote_copy(
             src_ref=fown.at[pl.ds(16 if side == 0 else 0, 16)], dst_ref=fhalo.at[side],
-            send_sem=fssem.at[side], recv_sem=frsem.at[side],
+            send_sem=fssem, recv_sem=frsem,
             device_id={"lat": after if side == 0 else ahead}, device_id_type=MESH,
         )
 
@@ -193,17 +198,16 @@
             one = recv[ph, c, 2 * g].astype(F32)
             two = recv[ph, c, 2 * g + 1].astype(F32)
             low = lanes_of(one.shape) < 64
-            hsend[hp, 0, c, g] = jnp.where(low, pltpu.roll(one, 64, 1), two).astype(BF16)
-            hsend[hp, 1, c, g] = jnp.where(low, one, pltpu.roll(two, 64, 1)).astype(BF16)
+            hsend[hp, c, 0, g] = jnp.where(low, pltpu.roll(one, 64, 1), two).astype(BF16)
+            hsend[hp, c, 1, g] = jnp.where(low, one, pltpu.roll(two, 64, 1)).astype(BF16)
         halo_copy(hp, 0, c).start()
         halo_copy(hp, 1, c).start()
 
     def to_modes(ph, hp, c):
-        halo_copy(hp, 0, c).wait_recv()
-        halo_copy(hp, 1, c).wait_recv()
+        all_of(hrecv.at[hp, c], hrsem.at[hp, c]).wait_recv()
         for g in range(PAIRS):
-            one = hrecv[hp, 0, c, g].astype(F32)
-            two = hrecv[hp, 1, c, g].astype(F32)
+            one = hrecv[hp, c, 0, g].astype(F32)
+            two = hrecv[hp, c, 1, g].astype(F32)
             low = lanes_of(one.shape) < 64
             halo[c, 2 * g] = jnp.where(low, one, pltpu.roll(two, 64, 1)).astype(BF16)
             halo[c, 2 * g + 1] = jnp.where(low, pltpu.roll(one, 64, 1), two).astype(BF16)
@@ -241,68 +245,51 @@
         block = dot(inv[c], banded[...]).astype(BF16)
         for q in range(LON):
             send[ph, c, q] = block[q * CUT : q * CUT + CUT]
-        start_exchange(ph, c)
 
     theirs = pl.multiple_of((1 - core) * HALF, HALF)
     other_core = {"lon": me + 1 - 2 * core}
     gain_rows = pl.ds(GAIN_AT, TILE)
 
     def core_copy(kind):
-        rows = pl.ds(0, DOWN_AT) if kind == 0 else pl.ds(DOWN_AT, HALF + TILE - DOWN_AT)
+        rows = pl.ds(0, TILE + DOWN_AT) if kind == 0 else pl.ds(TILE + DOWN_AT, HALF - DOWN_AT)
         return pltpu.make_async_remote_copy(
             src_ref=csend.at[rows], dst_ref=crecv.at[rows], send_sem=cssem.at[kind], recv_sem=crsem.at[kind],
             device_id=other_core, device_id_type=MESH,
         )
 
-    def core_gather(base, k):
-        rows = pl.ds(base + k * SHARE, SHARE)
-        return pltpu.make_async_remote_copy(
-            src_ref=fin.at[rows], dst_ref=fin.at[rows], send_sem=cssem.at[2 + k], recv_sem=crsem.at[2 + k],
+    def core_gather(k):
+        rows = pl.ds(mine + k * SHARE, SHARE)
+        return pltpu.make_async_remote_copy(
+            src_ref=fin.at[rows], dst_ref=fin.at[rows], send_sem=cssem.at[2], recv_sem=crsem.at[2],
             device_id=other_core, device_id_type=MESH,
         )
 
-    def plane_copy(kind, to, own):
+    def plane_scatter(to):
+        return pltpu.make_async_remote_copy(
+            src_ref=ps.at[to], dst_ref=pr.at[plane], send_sem=pssem.at[0], recv_sem=prsem.at[0],
+            device_id=plane_peer(to), device_id_type=MESH,
+        )
+
+    def plane_gather(s):
+        return pltpu.make_async_remote_copy(
+            src_ref=zall.at[pl.ds(0, SHARE)], dst_ref=fin.at[pl.ds(mine + plane * SHARE, SHARE)],
+            send_sem=pssem.at[1], recv_sem=prsem.at[1 + (PLANE - s - 1) // GROUP],
+            device_id=plane_peer(lax.rem(plane + s, PLANE)), device_id_type=MESH,
+        )
+
+    def z_copy(kind, to):
         src, dst = (
-            (ps.at[to], pr.at[own]),
-            (zall.at[pl.ds(0, SHARE)], fin.at[pl.ds(mine + own * SHARE, SHARE)]),
+            (zs.at[pl.ds(to * Z_ROWS, Z_ROWS)], zr.at[z]),
+            (zall.at[pl.ds(z * Z_ROWS, Z_ROWS)], zall.at[pl.ds(z * Z_ROWS, Z_ROWS)]),
         )[kind]
-        return src, dst
-
-    def z_copy(kind, to, own):
-        src, dst = (
-            (zs.at[pl.ds(to * Z_ROWS, Z_ROWS)], zr.at[own]),
-            (zall.at[pl.ds(own * Z_ROWS, Z_ROWS)], zall.at[pl.ds(own * Z_ROWS, Z_ROWS)]),
-        )[kind]
-        return src, dst
-
-    rings = {
-        "plane": (plane, PLANE, plane_copy, plane_peer, pssem, prsem),
-        "z": (z, 8, z_copy, z_peer, zssem, zrsem),
-    }
-
-    def ring_copy(axis, kind, to, own):
-        _, _, copy, peer, send_sems, recv_sems = rings[axis]
-        src, dst = copy(kind, to, own)
-        return pltpu.make_async_remote_copy(
-            src_ref=src, dst_ref=dst, send_sem=send_sems.at[kind, to], recv_sem=recv_sems.at[kind, own],
-            device_id=peer(to), device_id_type=MESH,
-        )
-
-    def ring_start(axis, kind):
-        here, count = rings[axis][:2]
-        for s in range(1, count):
-            ring_copy(axis, kind, lax.rem(here + s, count), here).start()
-
-    def ring_arrived(axis, kind):
-        here, count = rings[axis][:2]
-        for s in range(1, count):
-            there = lax.rem(here + s, count)
-            ring_copy(axis, kind, there, there).wait_recv()
-
-    def ring_sent(axis, kind):
-        here, count = rings[axis][:2]
-        for s in range(1, count):
-            ring_copy(axis, kind, lax.rem(here + s, count), here).wait_send()
+        return pltpu.make_async_remote_copy(
+            src_ref=src, dst_ref=dst, send_sem=zssem.at[kind], recv_sem=zrsem.at[kind],
+            device_id=z_peer(to), device_id_type=MESH,
+        )
+
+    def z_start(kind):
+        for s in range(1, 8):
+            z_copy(kind, lax.rem(z + s, 8)).start()
 
     def others(ref, here, count, rows):
         total = ref[lax.rem(here + 1, count), rows, :].astype(F32)
@@ -313,48 +300,55 @@
     def send_half(first, last):
         @pl.loop(first // 256, last // 256)
         def _(step):
-            csend[pl.ds(step * 256, 256), :] = part[pl.ds(theirs + step * 256, 256), :].astype(BF16)
-
-    def scatter_plane():
-        core_copy(0).wait_recv()
-        core_copy(1).wait_recv()
-        g = part[gain_rows, :] + crecv[HALF:, :].astype(F32)
-        part[gain_rows, :] = g
-
-        @pl.loop(0, PLANE)
+            csend[pl.ds(TILE + step * 256, 256), :] = part[pl.ds(theirs + step * 256, 256), :].astype(BF16)
+
+    def scatter_plane(half):
+        core_copy(half).wait_recv()
+        if half == 0:
+            part[gain_rows, :] += crecv[0:TILE, :].astype(F32)
+        g16 = part[gain_rows, :].astype(BF16)
+
+        @pl.loop(half * 8, half * 8 + 8)
         def _(to):
-            v = part[pl.ds(mine + to * SHARE, SHARE), :] + crecv[pl.ds(to * SHARE, SHARE), :].astype(F32)
-            part[pl.ds(mine + to * SHARE, SHARE), :] = v
+            rows = pl.ds(mine + to * SHARE, SHARE)
+            v = part[rows, :] + crecv[pl.ds(TILE + to * SHARE, SHARE), :].astype(F32)
+            part[rows, :] = v
             ps[to, 0:SHARE, :] = v.astype(BF16)
-            ps[to, SHARE:, :] = g.astype(BF16)
-
-        ring_start("plane", 0)
+            ps[to, SHARE:, :] = g16
+
+        for s in range(8):
+            to = half * 8 + lax.rem(plane + s, 8)
+
+            @pl.when(to != plane)
+            def _():
+                plane_scatter(to).start()
 
     def scatter_z():
-        ring_arrived("plane", 0)
+        all_of(pr.at[pl.ds(0, PLANE - 1)], prsem.at[0]).wait_recv()
         zf[SHARE + TILE :, :] = jnp.zeros((8 * Z_ROWS - SHARE - TILE, 128), F32)
         zf[0:SHARE, :] = part[pl.ds(mine + plane * SHARE, SHARE), :] + others(pr, plane, PLANE, pl.ds(0, SHARE))
         zf[SHARE : SHARE + TILE, :] = part[gain_rows, :] + others(pr, plane, PLANE, pl.ds(SHARE, TILE))
         zs[...] = zf[...].astype(BF16)
-        ring_start("z", 0)
+        z_start(0)
 
     def gather_z():
-        ring_arrived("z", 0)
+        all_of(zr.at[pl.ds(0, 7)], zrsem.at[0]).wait_recv()
         rows = pl.ds(pl.multiple_of(z * Z_ROWS, Z_ROWS), Z_ROWS)
         zall[rows, :] = (zf[rows, :] + others(zr, z, 8, pl.ds(0, Z_ROWS))).astype(BF16)
-        ring_start("z", 1)
+        z_start(1)
 
     def gather_plane():
-        ring_arrived("z", 1)
-        ring_start("plane", 1)
+        all_of(zall.at[pl.ds(0, 7 * Z_ROWS)], zrsem.at[1]).wait_recv()
+        for s in range(1, PLANE):
+            plane_gather(s).start()
         fin[pl.ds(mine + plane * SHARE, SHARE), :] = zall[0:SHARE, :]
-        core_gather(mine, plane).start()
+        core_gather(plane).start()
 
     def gather_core():
-        for s in range(1, PLANE):
-            there = lax.rem(plane + s, PLANE)
-            ring_copy("plane", 1, there, there).wait_recv()
-            core_gather(mine, there).start()
+        for group in range((PLANE - 1) // GROUP):
+            all_of(fin.at[pl.ds(0, GROUP * SHARE)], prsem.at[1 + group]).wait_recv()
+            for s in range(1 + group * GROUP, 1 + (group + 1) * GROUP):
+                core_gather(lax.rem(plane + s, PLANE)).start()
 
     gets[0].wait()
     for half in range(2):
@@ -373,6 +367,7 @@
 
     gets[1].wait()
     gets[2].wait()
+    gets[11].wait()
     fstage[...] = jnp.zeros_like(fstage)
     row = lax.broadcasted_iota(jnp.int32, (ROWS, NLON), 0)
     mode = lax.broadcasted_iota(jnp.int32, (ROWS, NLON), 1)
@@ -409,11 +404,12 @@
     gets[6].wait()
     for c in range(CHUNKS):
         to_grid(1, c)
-
-    for get in gets[7:]:
+        start_exchange(1, c)
+
+    for get in gets[7:11]:
         get.wait()
-    filter_copy(0).wait()
-    filter_copy(1).wait()
+    all_of(fhalo, fssem).wait_send()
+    all_of(fhalo, frsem).wait_recv()
 
     @pl.loop(0, MODES // 256)
     def _(step):
@@ -449,11 +445,10 @@
             u = before[at, :]
             u2 = u * u
             tangent = jnp.tanh(u * (SQRT_TWO_PI + (SQRT_TWO_PI * CUBIC) * u2))
-            h = 0.5 * u
-            hidden[at, :] = (h + h * tangent).astype(BF16)
-            slope = (0.5 + 0.5 * tangent) + (h * (1.0 - tangent * tangent)) * (
-                SQRT_TWO_PI + (3.0 * SQRT_TWO_PI * CUBIC) * u2
-            )
+            e = 0.5 * tangent + 0.5
+            value = u * e
+            hidden[at, :] = value.astype(BF16)
+            slope = e + value * (1.0 - e) * (2.0 * SQRT_TWO_PI + (6.0 * SQRT_TWO_PI * CUBIC) * u2)
             dbef[at, :] = (dhid[at, :] * slope).astype(BF16)
 
         field[all_rows, :] = dot_transpose(dbef[all_rows, :], wup[...])
@@ -465,7 +460,7 @@
             inverse = lax.rsqrt(jnp.mean(sf * sf, axis=-1, keepdims=True) + 1e-06)
             normed = sf * inverse
             d_scaled = field[at, :]
-            gsum[...] += jnp.sum(d_scaled * normed, axis=0, keepdims=True)
+            gsum[...] += jnp.sum((d_scaled * normed).reshape(16, 8, CH), axis=0)
             gained = d_scaled * gain[...]
             value = cflat[at, :].astype(F32) + inverse * (
                 gained - normed * jnp.mean(gained * normed, axis=-1, keepdims=True)
@@ -490,33 +485,35 @@
     for h in range(8):
         at = h // 4 * HALF + UP_AT + h % 4 * 256
         part[at : at + 256, :] = term[:, h * 128 : h * 128 + 128]
+    part[gain_rows, :] = jnp.zeros((TILE, 128), F32)
+    total = jnp.sum(gsum[...], axis=0, keepdims=True)
+    for h in range(2):
+        part[GAIN_AT + h : GAIN_AT + h + 1, :] = total[:, h * 128 : h * 128 + 128]
+    csend[0:TILE, :] = part[gain_rows, :].astype(BF16)
     send_half(0, DOWN_AT)
     core_copy(0).start()
     term = dot_rows(hidden[...], cflat[...])
     for h in range(2):
         part[h * HALF + DOWN_AT : (h + 1) * HALF, :] = term[:, h * 128 : h * 128 + 128]
-    part[gain_rows, :] = jnp.zeros((TILE, 128), F32)
-    for h in range(2):
-        part[GAIN_AT + h : GAIN_AT + h + 1, :] = gsum[:, h * 128 : h * 128 + 128]
     send_half(DOWN_AT, HALF)
-    csend[HALF:, :] = part[gain_rows, :].astype(BF16)
     core_copy(1).start()
-
+    scatter_plane(0)
+    scatter_plane(1)
     result = stream[...].astype(F32) + dot(hidden[...], wdown[...])
     res[...] = result[0 : ROWS * COLS].reshape(COLS, ROWS, CH).astype(BF16)
     put_out = pltpu.make_async_copy(res, out, osem.at[0])
     put_out.start()
-    scatter_plane()
 
     for c in range(CHUNKS):
         pass_halo(2, 1, c)
+    scatter_z()
     for c in range(CHUNKS):
         to_modes(2, 1, c)
-    scatter_z()
+    gather_z()
     band_sum(dcoef, 0, MODES // 128)
     for c in range(CHUNKS):
         to_grid(3, c)
-    gather_z()
+        start_exchange(3, c)
 
     def put_grad(half, rows, block):
         ds[half, rows, :] = block + ds[half, rows, :]
@@ -537,25 +534,20 @@
     put_other = pltpu.make_async_copy(fin.at[pl.ds(theirs, HALF)], sums.at[pl.ds(theirs, HALF)], osem.at[4])
     put_gain.start()
     put_own.start()
-    for k in range(PLANE):
-        core_gather(theirs, k).wait_recv()
+    all_of(fin.at[pl.ds(0, HALF)], crsem.at[2]).wait_recv()
     put_other.start()
 
     core_copy(0).wait_send()
     core_copy(1).wait_send()
-    for k in range(PLANE):
-        core_gather(mine, k).wait_send()
+    all_of(fin.at[pl.ds(0, HALF)], cssem.at[2]).wait_send()
+    all_of(ps.at[pl.ds(0, PLANE - 1)], pssem.at[0]).wait_send()
+    all_of(fin.at[pl.ds(0, (PLANE - 1) * SHARE)], pssem.at[1]).wait_send()
     for kind in range(2):
-        ring_sent("plane", kind)
-        ring_sent("z", kind)
+        all_of(zs.at[pl.ds(0, 7 * Z_ROWS)], zssem.at[kind]).wait_send()
     for ph in range(4):
-        for c in range(CHUNKS):
-            for s in range(1, LON):
-                exchange(ph, c, lax.rem(me + s, LON), me).wait_send()
+        all_of(send.at[ph, :, pl.ds(0, LON - 1)], ssem.at[ph]).wait_send()
     for hp in range(2):
-        for c in range(CHUNKS):
-            halo_copy(hp, 0, c).wait_send()
-            halo_copy(hp, 1, c).wait_send()
+        all_of(hsend.at[hp], hssem.at[hp]).wait_send()
     put_out.wait()
     put_grad_out.wait()
     put_gain.wait()
@@ -563,31 +555,46 @@
     put_other.wait()
 
 
-def finish(res, gres, sums, out, grad, mix_o, gain_o, up_o, down_o):
-    out[...] = res[...]
-    grad[...] = gres[...]
+def finish(res, gres, sums, out, grad, mix_o, gain_o, up_o, down_o, first, second, half, mix, gain, up, down, sem):
+    fields = [pltpu.make_async_copy(res, first, sem.at[0]), pltpu.make_async_copy(gres, second, sem.at[1])]
+    puts = [pltpu.make_async_copy(first, out, sem.at[4]), pltpu.make_async_copy(second, grad, sem.at[5])]
+    gets = [
+        pltpu.make_async_copy(
+            sums.at[pl.ds(h * HALF, HALF + h * TILE)], half.at[pl.ds(h * HALF, HALF + h * TILE)], sem.at[2 + h]
+        )
+        for h in range(2)
+    ]
+    for copy in gets + fields:
+        copy.start()
     for h in range(2):
+        gets[h].wait()
         lanes = slice(h * 128, h * 128 + 128)
         at = h * HALF
-        mix_o[:, lanes] = sums[at : at + UP_AT, :].astype(F32) * NORM_SCALE
-        down_o[:, lanes] = sums[at + DOWN_AT : at + HALF, :].astype(F32) * NORM_SCALE
-        gain_o[:, lanes] = sums[GAIN_AT : GAIN_AT + TILE, :].astype(F32)[h : h + 1, :] * NORM_SCALE
-    for h in range(8):
-        at = h // 4 * HALF + UP_AT + h % 4 * 256
-        up_o[:, h * 128 : h * 128 + 128] = sums[at : at + 256, :].astype(F32) * NORM_SCALE
+        mix[:, lanes] = half[at : at + UP_AT, :].astype(F32) * NORM_SCALE
+        for b in range(4):
+            start = at + UP_AT + b * 256
+            up[:, h * 512 + b * 128 : h * 512 + b * 128 + 128] = half[start : start + 256, :].astype(F32) * NORM_SCALE
+        down[:, lanes] = half[at + DOWN_AT : at + HALF, :].astype(F32) * NORM_SCALE
+        fields[h].wait()
+        puts[h].start()
+    for h in range(2):
+        gain[:, h * 128 : h * 128 + 128] = half[GAIN_AT : GAIN_AT + TILE, :].astype(F32)[h : h + 1, :] * NORM_SCALE
+    for k, (src, dst) in enumerate(((up, up_o), (down, down_o), (mix, mix_o), (gain, gain_o))):
+        puts.append(pltpu.make_async_copy(src, dst, sem.at[6 + k]))
+        puts[-1].start()
+    for copy in puts:
+        copy.wait()
 
 
 def local(grid_in, grid_cotangent, support_filter, band_half, w_mix, norm_gain, w_up, w_down):
     forward, inverse = fourier_tables()
     efwd, ebwd = expansion()
-    vmem = pl.BlockSpec(memory_space=pltpu.VMEM)
-    smem = pl.BlockSpec(memory_space=pltpu.SMEM)
     anywhere = pl.BlockSpec(memory_space=pl.ANY)
     field = jax.ShapeDtypeStruct((COLS, ROWS, CH), BF16)
     res, gres, sums = pl.pallas_call(
         kernel,
         out_shape=(field, field, jax.ShapeDtypeStruct((2 * HALF + TILE, 128), BF16)),
-        in_specs=[anywhere] * 3 + [smem] + [anywhere] * 8,
+        in_specs=[anywhere] * 12,
         out_specs=[anywhere] * 3,
         scratch_shapes=[
             pltpu.VMEM((CHUNKS, MODES, WIDE), BF16),
@@ -596,8 +603,8 @@
             pltpu.VMEM((FLAT, CH), BF16),
             pltpu.VMEM((4, CHUNKS, LON, CUT, 128), BF16),
             pltpu.VMEM((4, CHUNKS, LON, CUT, 128), BF16),
-            pltpu.VMEM((2, 2, CHUNKS, PAIRS, CUT, 128), BF16),
-            pltpu.VMEM((2, 2, CHUNKS, PAIRS, CUT, 128), BF16),
+            pltpu.VMEM((2, CHUNKS, 2, PAIRS, CUT, 128), BF16),
+            pltpu.VMEM((2, CHUNKS, 2, PAIRS, CUT, 128), BF16),
             pltpu.VMEM((CHUNKS, LON, CUT, 128), BF16),
             pltpu.VMEM((32, MODES), F32),
             pltpu.VMEM((32, MODES), BF16),
@@ -619,7 +626,7 @@
             pltpu.VMEM((FLAT, CH), BF16),
             pltpu.VMEM((COLS, ROWS, CH), BF16),
             pltpu.VMEM((COLS, ROWS, CH), BF16),
-            pltpu.VMEM((1, CH), F32),
+            pltpu.VMEM((8, CH), F32),
             pltpu.VMEM((2 * HALF + TILE, 128), F32),
             pltpu.VMEM((HALF + TILE, 128), BF16),
             pltpu.VMEM((HALF + TILE, 128), BF16),
@@ -633,26 +640,27 @@
             pltpu.VMEM((COLS, ROWS, CH), BF16),
             pltpu.VMEM((COLS, ROWS, CH), BF16),
             pltpu.VMEM((TAPS, ROWS, NLON), F32),
+            pltpu.SMEM((ROWS,), jnp.int32),
             pltpu.VMEM((CH, CH), BF16),
             pltpu.VMEM((1, CH), F32),
             pltpu.VMEM((CH, HID), BF16),
             pltpu.VMEM((HID, CH), BF16),
             pltpu.VMEM((32, TAPS * 128), BF16),
             pltpu.VMEM((64, TAPS * 128), BF16),
-            pltpu.SemaphoreType.DMA((11,)),
+            pltpu.SemaphoreType.DMA((12,)),
             pltpu.SemaphoreType.DMA((5,)),
-            pltpu.SemaphoreType.DMA((4, CHUNKS, LON)),
-            pltpu.SemaphoreType.DMA((4, CHUNKS, LON)),
-            pltpu.SemaphoreType.DMA((2, 2, CHUNKS)),
-            pltpu.SemaphoreType.DMA((2, 2, CHUNKS)),
+            pltpu.SemaphoreType.DMA((4,)),
+            pltpu.SemaphoreType.DMA((4, CHUNKS)),
+            pltpu.SemaphoreType.DMA((2,)),
+            pltpu.SemaphoreType.DMA((2, CHUNKS)),
+            pltpu.SemaphoreType.DMA,
+            pltpu.SemaphoreType.DMA,
+            pltpu.SemaphoreType.DMA((3,)),
+            pltpu.SemaphoreType.DMA((3,)),
+            pltpu.SemaphoreType.DMA((2,)),
+            pltpu.SemaphoreType.DMA((1 + (PLANE - 1) // GROUP,)),
             pltpu.SemaphoreType.DMA((2,)),
             pltpu.SemaphoreType.DMA((2,)),
-            pltpu.SemaphoreType.DMA((2 + PLANE,)),
-            pltpu.SemaphoreType.DMA((2 + PLANE,)),
-            pltpu.SemaphoreType.DMA((2, PLANE)),
-            pltpu.SemaphoreType.DMA((2, PLANE)),
-            pltpu.SemaphoreType.DMA((2, 8)),
-            pltpu.SemaphoreType.DMA((2, 8)),
         ],
         compiler_params=pltpu.CompilerParams(
             collective_id=0, has_side_effects=True, vmem_limit_bytes=60 * 1024 * 1024
@@ -673,8 +681,18 @@
             jax.ShapeDtypeStruct((CH, HID), F32),
             jax.ShapeDtypeStruct((HID, CH), F32),
         ),
-        in_specs=[vmem] * 3,
-        out_specs=[vmem] * 6,
+        in_specs=[anywhere] * 3,
+        out_specs=[anywhere] * 6,
+        scratch_shapes=[
+            pltpu.VMEM((COLS, ROWS, CH), BF16),
+            pltpu.VMEM((COLS, ROWS, CH), BF16),
+            pltpu.VMEM((2 * HALF + TILE, 128), BF16),
+            pltpu.VMEM((CH, CH), F32),
+            pltpu.VMEM((1, CH), F32),
+            pltpu.VMEM((CH, HID), F32),
+            pltpu.VMEM((HID, CH), F32),
+            pltpu.SemaphoreType.DMA((10,)),
+        ],
         compiler_params=pltpu.CompilerParams(vmem_limit_bytes=60 * 1024 * 1024),
     )(res, gres, sums)
     return (

time: 102 us -> 89.8 us (0.88)
  Pallas kernels: 101 us -> 89.1 us
    pallas_call x1, Pallas kernels: 97.8 us -> 86 us  [local(): pl.pallas_call(kernel, out_shape=(field, field, jax.ShapeDtypeStruct((2 *...]
where the time goes in v4:
time: 89.8 us; the launch traced here: 89.7 us
  Pallas kernels  89.1 us (99%)
    pallas_call x1, Pallas kernels, local(): pl.pallas_call(kernel, out_shape=(field, field, jax.ShapeDtypeStruct((2 *...  86 us
    pallas_call x1, Pallas kernels, local(): pl.pallas_call(finish, out_shape=(field, field, jax.ShapeDtypeStruct((CH,...  3.07 us

profile of v4, /device:TPU:1, one launch (start us, length us, event | category | flops | bytes accessed | tf_op | source)
XLA Modules:
  0.0 89.7 jit_solution(375235366622183086)
XLA Ops:
  0.6 86.0 %shard_map.163 = (bf16[180,4,256]{2,1,0:T(4,128)(2,1)}, bf16[180,4,256]{2,1,0:T(4,128)(2,1)}, bf16[4624,128]{1,0:T(8,128)(2,1)}) custom-call(bf16[180,4,256]{2,1,0:T(4,128)(2,1)} %bitcast.7, bf16[180,4,256]{2,1,0:T(4,128)(2,1)} %bitcast.8, f32[5,4,1440]{2,1,0:T(4,128)} %bitcast.11, s32[4]{0:T(128)} %band_hbm.1, bf16[256,256]{1,0:T(8,128)(2,1)} %wmix_hbm.1, ...), custom_call_target="tpu_custom_call" | custom-call | flops 4700000256 | bytes 14000000 | tf_op jit(solution)/shard_map/pallas_call | solution.py:594
  86.6 3.1 %shard_map.164 = (bf16[180,4,256]{2,1,0:T(4,128)(2,1)}, bf16[180,4,256]{2,1,0:T(4,128)(2,1)}, f32[256,256]{1,0:T(8,128)}, f32[1,256]{1,0:T(1,128)}, f32[256,1024]{1,0:T(8,128)}, /*index=5*/f32[1024,256]{1,0:T(8,128)}) custom-call(bf16[180,4,256]{2,1,0:T(4,128)(2,1)} %get-tuple-element.15.res, bf16[180,4,256]{2,1,0:T(4,128)(2,1)} %get-tuple-element.16.gres, ...), custom_call_target="tpu_custom_call" | custom-call | tf_op jit(solution)/shard_map/pallas_call | solution.py:674

commit v5 on v4

--- a/solution.py
+++ b/solution.py
@@ -29,6 +29,9 @@
 TAPS = 5
 FLAT = ROWS * BLK
 PART = ROWS * CUT
+BAND_STEP = 512
+NORM_STEP = 256
+GELU_STEP = 32
 
 HALF = 2304
 UP_AT, DOWN_AT = 256, 1280
@@ -221,10 +224,10 @@
             term = dot(fwd[c, at, :], both)
             spec[at, :] = term if c == 0 else spec[at, :] + term
 
-    def band_sum(weights, first, last):
-        @pl.loop(first, last)
+    def band_sum(weights):
+        @pl.loop(0, MODES // BAND_STEP)
         def _(step):
-            at = pl.ds(pl.multiple_of(step * 128, 128), 128)
+            at = pl.ds(pl.multiple_of(step * BAND_STEP, BAND_STEP), BAND_STEP)
             own = spec[at, 0:128]
             edge = spec[at, 128:256]
             lane = lanes_of(own.shape)
@@ -400,7 +403,7 @@
     gets[5].wait()
     for c in range(CHUNKS):
         to_modes(0, 0, c)
-    band_sum(coef, 0, MODES // 128)
+    band_sum(coef)
     gets[6].wait()
     for c in range(CHUNKS):
         to_grid(1, c)
@@ -427,9 +430,9 @@
         conv[all_rows, :] = jnp.concatenate([cf[0, all_rows, :], cf[1, all_rows, :]], axis=1).astype(BF16)
         field[all_rows, :] = dot(conv[all_rows, :], wmix[...])
 
-        @pl.loop(0, PART // 128)
+        @pl.loop(0, PART // NORM_STEP)
         def _(step):
-            at = pl.ds(c * PART + step * 128, 128)
+            at = pl.ds(c * PART + step * NORM_STEP, NORM_STEP)
             mixed = field[at, :] + jnp.concatenate([gf[0, at, :], gf[1, at, :]], axis=1)
             s16 = mixed.astype(BF16)
             stream[at, :] = s16
@@ -439,9 +442,9 @@
 
         before[all_rows, :] = dot(scaled[all_rows, :], wup[...])
 
-        @pl.loop(0, PART // 16)
+        @pl.loop(0, PART // GELU_STEP)
         def _(step):
-            at = pl.ds(c * PART + step * 16, 16)
+            at = pl.ds(c * PART + step * GELU_STEP, GELU_STEP)
             u = before[at, :]
             u2 = u * u
             tangent = jnp.tanh(u * (SQRT_TWO_PI + (SQRT_TWO_PI * CUBIC) * u2))
@@ -453,14 +456,14 @@
 
         field[all_rows, :] = dot_transpose(dbef[all_rows, :], wup[...])
 
-        @pl.loop(0, PART // 128)
+        @pl.loop(0, PART // NORM_STEP)
         def _(step):
-            at = pl.ds(c * PART + step * 128, 128)
+            at = pl.ds(c * PART + step * NORM_STEP, NORM_STEP)
             sf = stream[at, :].astype(F32)
             inverse = lax.rsqrt(jnp.mean(sf * sf, axis=-1, keepdims=True) + 1e-06)
             normed = sf * inverse
             d_scaled = field[at, :]
-            gsum[...] += jnp.sum((d_scaled * normed).reshape(16, 8, CH), axis=0)
+            gsum[...] += jnp.sum((d_scaled * normed).reshape(NORM_STEP // 8, 8, CH), axis=0)
             gained = d_scaled * gain[...]
             value = cflat[at, :].astype(F32) + inverse * (
                 gained - normed * jnp.mean(gained * normed, axis=-1, keepdims=True)
@@ -510,7 +513,7 @@
     for c in range(CHUNKS):
         to_modes(2, 1, c)
     gather_z()
-    band_sum(dcoef, 0, MODES // 128)
+    band_sum(dcoef)
     for c in range(CHUNKS):
         to_grid(3, c)
         start_exchange(3, c)

time: 89.8 us -> 87.4 us (0.973)
  Pallas kernels: 89.1 us -> 86.7 us
    pallas_call x1, Pallas kernels: 86 us -> 83.6 us  [local(): pl.pallas_call(kernel, out_shape=(field, field, jax.ShapeDtypeStruct((2 *...]
where the time goes in v5:
time: 87.4 us; the launch traced here: 87.3 us
  Pallas kernels  86.7 us (99%)
    pallas_call x1, Pallas kernels, local(): pl.pallas_call(kernel, out_shape=(field, field, jax.ShapeDtypeStruct((2 *...  83.6 us
    pallas_call x1, Pallas kernels, local(): pl.pallas_call(finish, out_shape=(field, field, jax.ShapeDtypeStruct((CH,...  3.07 us

profile of v5, /device:TPU:1, one launch (start us, length us, event | category | flops | bytes accessed | tf_op | source)
XLA Modules:
  0.0 87.3 jit_solution(360680938557825565)
XLA Ops:
  0.6 83.6 %shard_map.163 = (bf16[180,4,256]{2,1,0:T(4,128)(2,1)}, bf16[180,4,256]{2,1,0:T(4,128)(2,1)}, bf16[4624,128]{1,0:T(8,128)(2,1)}) custom-call(bf16[180,4,256]{2,1,0:T(4,128)(2,1)} %bitcast.7, bf16[180,4,256]{2,1,0:T(4,128)(2,1)} %bitcast.8, f32[5,4,1440]{2,1,0:T(4,128)} %bitcast.11, s32[4]{0:T(128)} %band_hbm.1, bf16[256,256]{1,0:T(8,128)(2,1)} %wmix_hbm.1, ...), custom_call_target="tpu_custom_call" | custom-call | flops 4700000256 | bytes 14000000 | tf_op jit(solution)/shard_map/pallas_call | solution.py:597
  84.2 3.1 %shard_map.164 = (bf16[180,4,256]{2,1,0:T(4,128)(2,1)}, bf16[180,4,256]{2,1,0:T(4,128)(2,1)}, f32[256,256]{1,0:T(8,128)}, f32[1,256]{1,0:T(1,128)}, f32[256,1024]{1,0:T(8,128)}, /*index=5*/f32[1024,256]{1,0:T(8,128)}) custom-call(bf16[180,4,256]{2,1,0:T(4,128)(2,1)} %get-tuple-element.15.res, bf16[180,4,256]{2,1,0:T(4,128)(2,1)} %get-tuple-element.16.gres, ...), custom_call_target="tpu_custom_call" | custom-call | tf_op jit(solution)/shard_map/pallas_call | solution.py:677

commit v6 on v5

--- a/solution.py
+++ b/solution.py
@@ -31,7 +31,7 @@
 PART = ROWS * CUT
 BAND_STEP = 512
 NORM_STEP = 256
-GELU_STEP = 32
+GELU_STEP = 64
 
 HALF = 2304
 UP_AT, DOWN_AT = 256, 1280
@@ -206,7 +206,7 @@
         halo_copy(hp, 0, c).start()
         halo_copy(hp, 1, c).start()
 
-    def to_modes(ph, hp, c):
+    def lay_halo(hp, c):
         all_of(hrecv.at[hp, c], hrsem.at[hp, c]).wait_recv()
         for g in range(PAIRS):
             one = hrecv[hp, c, 0, g].astype(F32)
@@ -215,14 +215,18 @@
             halo[c, 2 * g] = jnp.where(low, one, pltpu.roll(two, 64, 1)).astype(BF16)
             halo[c, 2 * g + 1] = jnp.where(low, pltpu.roll(one, 64, 1), two).astype(BF16)
 
+    def to_modes(ph, chunks):
         @pl.loop(0, MODES // 512)
         def _(step):
             at = pl.ds(pl.multiple_of(step * 512, 512), 512)
-            both = jnp.concatenate(
-                [recv[ph, c].reshape(WIDE, 128), halo[c].reshape(WIDE, 128)], axis=1
-            )
-            term = dot(fwd[c, at, :], both)
-            spec[at, :] = term if c == 0 else spec[at, :] + term
+            total = None if chunks[0] == 0 else spec[at, :]
+            for c in chunks:
+                both = jnp.concatenate(
+                    [recv[ph, c].reshape(WIDE, 128), halo[c].reshape(WIDE, 128)], axis=1
+                )
+                term = dot(fwd[c, at, :], both)
+                total = term if total is None else total + term
+            spec[at, :] = total
 
     def band_sum(weights):
         @pl.loop(0, MODES // BAND_STEP)
@@ -402,7 +406,8 @@
         pass_halo(0, 0, c)
     gets[5].wait()
     for c in range(CHUNKS):
-        to_modes(0, 0, c)
+        lay_halo(0, c)
+        to_modes(0, [c])
     band_sum(coef)
     gets[6].wait()
     for c in range(CHUNKS):
@@ -511,9 +516,10 @@
         pass_halo(2, 1, c)
     scatter_z()
     for c in range(CHUNKS):
-        to_modes(2, 1, c)
+        lay_halo(1, c)
+    to_modes(2, list(range(CHUNKS)))
+    band_sum(dcoef)
     gather_z()
-    band_sum(dcoef)
     for c in range(CHUNKS):
         to_grid(3, c)
         start_exchange(3, c)

time: 87.4 us -> 87.2 us (level)
  no operation moved by 1% of the time
where the time goes in v6:
time: 87.2 us; the launch traced here: 87.1 us
  Pallas kernels  86.5 us (99%)
    pallas_call x1, Pallas kernels, local(): pl.pallas_call(kernel, out_shape=(field, field, jax.ShapeDtypeStruct((2 *...  83.4 us
    pallas_call x1, Pallas kernels, local(): pl.pallas_call(finish, out_shape=(field, field, jax.ShapeDtypeStruct((CH,...  3.07 us

profile of v6, /device:TPU:1, one launch (start us, length us, event | category | flops | bytes accessed | tf_op | source)
XLA Modules:
  0.0 87.1 jit_solution(15444276514045028752)
XLA Ops:
  0.6 83.4 %shard_map.163 = (bf16[180,4,256]{2,1,0:T(4,128)(2,1)}, bf16[180,4,256]{2,1,0:T(4,128)(2,1)}, bf16[4624,128]{1,0:T(8,128)(2,1)}) custom-call(bf16[180,4,256]{2,1,0:T(4,128)(2,1)} %bitcast.7, bf16[180,4,256]{2,1,0:T(4,128)(2,1)} %bitcast.8, f32[5,4,1440]{2,1,0:T(4,128)} %bitcast.11, s32[4]{0:T(128)} %band_hbm.1, bf16[256,256]{1,0:T(8,128)(2,1)} %wmix_hbm.1, ...), custom_call_target="tpu_custom_call" | custom-call | flops 4700000256 | bytes 14000000 | tf_op jit(solution)/shard_map/pallas_call | solution.py:603
  84.1 3.1 %shard_map.164 = (bf16[180,4,256]{2,1,0:T(4,128)(2,1)}, bf16[180,4,256]{2,1,0:T(4,128)(2,1)}, f32[256,256]{1,0:T(8,128)}, f32[1,256]{1,0:T(1,128)}, f32[256,1024]{1,0:T(8,128)}, /*index=5*/f32[1024,256]{1,0:T(8,128)}) custom-call(bf16[180,4,256]{2,1,0:T(4,128)(2,1)} %get-tuple-element.15.res, bf16[180,4,256]{2,1,0:T(4,128)(2,1)} %get-tuple-element.16.gres, ...), custom_call_target="tpu_custom_call" | custom-call | tf_op jit(solution)/shard_map/pallas_call | solution.py:683

commit v7 on v6

--- a/solution.py
+++ b/solution.py
@@ -507,13 +507,12 @@
     core_copy(1).start()
     scatter_plane(0)
     scatter_plane(1)
+    for c in range(CHUNKS):
+        pass_halo(2, 1, c)
     result = stream[...].astype(F32) + dot(hidden[...], wdown[...])
     res[...] = result[0 : ROWS * COLS].reshape(COLS, ROWS, CH).astype(BF16)
     put_out = pltpu.make_async_copy(res, out, osem.at[0])
     put_out.start()
-
-    for c in range(CHUNKS):
-        pass_halo(2, 1, c)
     scatter_z()
     for c in range(CHUNKS):
         lay_halo(1, c)
@@ -528,6 +527,7 @@
         ds[half, rows, :] = block + ds[half, rows, :]
 
     gather_plane()
+    gather_core()
     for c in range(CHUNKS):
         arrived(3, c)
         unpack(3, c, put_grad)
@@ -537,7 +537,6 @@
         gres[c * CUT : c * CUT + count] = both.reshape(count, ROWS, CH).astype(BF16)
     put_grad_out = pltpu.make_async_copy(gres, grad, osem.at[1])
     put_grad_out.start()
-    gather_core()
     put_gain = pltpu.make_async_copy(zall.at[pl.ds(SHARE, TILE)], sums.at[pl.ds(GAIN_AT, TILE)], osem.at[2])
     put_own = pltpu.make_async_copy(fin.at[pl.ds(mine, HALF)], sums.at[pl.ds(mine, HALF)], osem.at[3])
     put_other = pltpu.make_async_copy(fin.at[pl.ds(theirs, HALF)], sums.at[pl.ds(theirs, HALF)], osem.at[4])

time: 87.2 us -> 86.8 us (level)
  no operation moved by 1% of the time
where the time goes in v7:
time: 86.8 us; the launch traced here: 86.7 us
  Pallas kernels  86.1 us (99%)
    pallas_call x1, Pallas kernels, local(): pl.pallas_call(kernel, out_shape=(field, field, jax.ShapeDtypeStruct((2 *...  83 us
    pallas_call x1, Pallas kernels, local(): pl.pallas_call(finish, out_shape=(field, field, jax.ShapeDtypeStruct((CH,...  3.07 us

profile of v7, /device:TPU:1, one launch (start us, length us, event | category | flops | bytes accessed | tf_op | source)
XLA Modules:
  0.0 86.7 jit_solution(17231344476068798761)
XLA Ops:
  0.6 83.0 %shard_map.163 = (bf16[180,4,256]{2,1,0:T(4,128)(2,1)}, bf16[180,4,256]{2,1,0:T(4,128)(2,1)}, bf16[4624,128]{1,0:T(8,128)(2,1)}) custom-call(bf16[180,4,256]{2,1,0:T(4,128)(2,1)} %bitcast.7, bf16[180,4,256]{2,1,0:T(4,128)(2,1)} %bitcast.8, f32[5,4,1440]{2,1,0:T(4,128)} %bitcast.11, s32[4]{0:T(128)} %band_hbm.1, bf16[256,256]{1,0:T(8,128)(2,1)} %wmix_hbm.1, ...), custom_call_target="tpu_custom_call" | custom-call | flops 4700000256 | bytes 14000000 | tf_op jit(solution)/shard_map/pallas_call | solution.py:602
  83.6 3.1 %shard_map.164 = (bf16[180,4,256]{2,1,0:T(4,128)(2,1)}, bf16[180,4,256]{2,1,0:T(4,128)(2,1)}, f32[256,256]{1,0:T(8,128)}, f32[1,256]{1,0:T(1,128)}, f32[256,1024]{1,0:T(8,128)}, /*index=5*/f32[1024,256]{1,0:T(8,128)}) custom-call(bf16[180,4,256]{2,1,0:T(4,128)(2,1)} %get-tuple-element.15.res, bf16[180,4,256]{2,1,0:T(4,128)(2,1)} %get-tuple-element.16.gres, ...), custom_call_target="tpu_custom_call" | custom-call | tf_op jit(solution)/shard_map/pallas_call | solution.py:682
